TPU v7x, 512 devices: a whole 4x8x8 slice. The times are simulated.
512 devices in a mesh: space: 128 (over z, y, core), mode: 4 (over x).
Axes of the slice: x: 4, y: 8, z: 8, core: 2. Of those that a mesh axis runs over, the one named last changes fastest.
Arguments:
- right_side: float32 [4, 2, 7, 262144], P('mode', None, None, 'space')
- jacobian: float32 [2, 7, 7, 7, 4096], P(None, None, None, None, 'space'), may hold values from -0.9 to 0.9
- neighbor_cols: int32 [6, 4096], P(None, 'space'), may hold values from 0 to 63
- halo_list: int32 [2048], P('space'), may hold values from 0 to 31
- iface_blocks: int32 [16384], P('space'), may hold values from 0 to 31
- iface_slot: int32 [16384], P('space'), may hold values from 0 to 255, as said below
- recv_target: int32 [32768], P('space'), may hold values from 0 to 32, as said below
- phase_map: int32 [4, 16384], P('mode', 'space'), may hold values from 0 to 35
- mortar: float32 [8192, 64], P('space'), may hold values from -0.75 to 0.75
Outputs:
- basis: float32 [4, 4, 2, 7, 262144], P(None, 'mode', None, None, 'space')
- hess: float32 [2, 4, 3], replicated
Inputs may be any that keep to these rules, and one draw needn't show every extreme that they name: `iface_slot`: each device's rows name distinct slots, never of its own reader index; each device fills all 2 slots of one other reader device drawn from the seed, and at most 2 rows go from one device to one reader. `recv_target`: consistent with iface_slot: a slot that no row fills holds 32.
All inputs are finite; a program needn't handle non-finite values.
Results may differ from a plain program's by a relative error of at most 0.0005.
Values sent between devices are 32-bit elements; how exact they have to be, the bound alone decides.
A program may use at most 64 MiB of HBM per device.

v0:
```python
import math

import jax
import jax.numpy as jnp
from jax import lax
from jax.sharding import PartitionSpec as P

FIELDS = 7
BLK = 64
HB = 16
KRY = 3
NPHASE = 36


HIGH = lax.Precision.HIGHEST
SHIFT = 2.0
OMEGA = 0.5
EPS = 1e-06


def padded(block, sides, width):
    for axis, dim in sides:
        count = lax.axis_size(axis)
        forward = [(i, i + 1) for i in range(count - 1)]
        backward = [(target, source) for source, target in forward]
        low = lax.ppermute(
            lax.slice_in_dim(block, block.shape[dim] - width, None, axis=dim), axis, forward
        )
        high = lax.ppermute(lax.slice_in_dim(block, 0, width, axis=dim), axis, backward)
        block = jnp.concatenate([low, block, high], axis=dim)
    return block


def apply_blocks(jacobian, gathered):
    real_part = jnp.einsum("oikb,ikbc->obc", jacobian[0], gathered[0], precision=HIGH) - jnp.einsum(
        "oikb,ikbc->obc", jacobian[1], gathered[1], precision=HIGH
    )
    imag_part = jnp.einsum("oikb,ikbc->obc", jacobian[0], gathered[1], precision=HIGH) + jnp.einsum(
        "oikb,ikbc->obc", jacobian[1], gathered[0], precision=HIGH
    )
    return jnp.stack([real_part, imag_part])


def shifted_self(level, blocks):
    omega = OMEGA * level
    return jnp.stack([SHIFT * blocks[0] - omega * blocks[1], SHIFT * blocks[1] + omega * blocks[0]])


def rotate_rows(level, offsets, rows):
    angle = level * offsets.astype(jnp.float32) * (2.0 * math.pi / NPHASE)
    cosine = jnp.cos(angle)[None, :, None]
    sine = jnp.sin(angle)[None, :, None]
    return jnp.stack([cosine * rows[0] - sine * rows[1], sine * rows[0] + cosine * rows[1]])


def local_inner(left, right):
    return jnp.stack(
        [
            jnp.sum(left[0] * right[0] + left[1] * right[1]),
            jnp.sum(left[0] * right[1] - left[1] * right[0]),
        ]
    )


def subtract(image, factor, vector):
    return image - jnp.stack(
        [
            factor[0] * vector[0] - factor[1] * vector[1],
            factor[0] * vector[1] + factor[1] * vector[0],
        ]
    )


def local(
    right_side,
    jacobian,
    neighbor_cols,
    halo_list,
    iface_blocks,
    iface_slot,
    recv_target,
    phase_map,
    mortar,
):
    nblk = neighbor_cols.shape[1]
    cells = right_side.shape[3]
    spread = lax.axis_size("space")
    slots = recv_target.shape[0]
    capacity = slots // spread
    count = jnp.float32(spread * lax.axis_size("mode") * cells)
    level = (lax.axis_index("mode") + 1).astype(jnp.float32)
    all_cols = jnp.concatenate([jnp.arange(nblk, dtype=jnp.int32)[None], neighbor_cols], 0)
    width = HB * BLK
    row_width = 2 * FIELDS * BLK
    forcing = right_side[0]
    first = jnp.sqrt(lax.psum(jnp.sum(forcing * forcing), ("space", "mode")) / count + EPS)
    vectors = [forcing / first]
    hess = jnp.zeros((2, KRY + 1, KRY), jnp.float32)
    for step in range(KRY):
        blocks = vectors[step].reshape(2, FIELDS, nblk, BLK)
        outgoing = blocks[:, :, halo_list, :].reshape(2, FIELDS, width)
        extended = padded(outgoing, (("space", 2),), width)
        before = extended[:, :, :width].reshape(2, FIELDS, HB, BLK)
        after = extended[:, :, 2 * width :].reshape(2, FIELDS, HB, BLK)
        matvec_rows = rotate_rows(level, phase_map[0], blocks[:, :, iface_blocks, :])
        packed = jnp.moveaxis(matvec_rows, 2, 0).reshape(matvec_rows.shape[2], row_width)
        buffer = (
            jnp.zeros((slots, row_width), jnp.float32)
            .at[iface_slot]
            .set(packed)
            .reshape(spread, capacity, row_width)
        )
        items = lax.all_to_all(buffer, "space", split_axis=0, concat_axis=0, tiled=True)
        lead, number, size = items.shape
        flat = items.reshape(lead * number * 2 * FIELDS, BLK)
        arrived = jnp.dot(flat, mortar, precision=HIGH, preferred_element_type=jnp.float32).reshape(
            lead, number, size
        )
        full = jnp.concatenate([blocks, before, after], 2)
        gathered = full[:, :, all_cols, :]
        result = apply_blocks(jacobian, gathered) + shifted_self(level, blocks)
        arrived = arrived.reshape(slots, 2, FIELDS, BLK)
        added = jax.ops.segment_sum(arrived, recv_target, num_segments=nblk + 1)[:nblk]
        result = result + jnp.moveaxis(added, 0, 2)
        image = result.reshape(2, FIELDS, cells)
        for index in range(step + 1):
            factor = lax.psum(local_inner(vectors[index], image), ("space", "mode")) / count
            image = subtract(image, factor, vectors[index])
            hess = hess.at[:, index, step].set(factor)
        length = jnp.sqrt(lax.psum(jnp.sum(image * image), ("space", "mode")) / count + EPS)
        hess = hess.at[0, step + 1, step].set(length)
        vectors.append(image / length)
    return (jnp.stack(vectors)[:, None], hess)


def solution(mesh):
    return jax.shard_map(
        local,
        mesh=mesh,
        in_specs=(
            P("mode", None, None, "space"),
            P(None, None, None, None, "space"),
            P(None, "space"),
            P("space"),
            P("space"),
            P("space"),
            P("space"),
            P("mode", "space"),
            P("space", None),
        ),
        out_specs=(P(None, "mode", None, None, "space"), P()),
        check_vma=False,
    )
```

profile of v0, /device:TPU:1, one launch (start us, length us, event | category | flops | bytes accessed | tf_op | source)
XLA Modules:
  0.0 1303.9 jit_solution(895305620957128106)
XLA Ops:
  0.6 1.6 multiply_reduce_fusion.2
  2.3 106.1 %psum.70 = f32[]{:T(128)} all-reduce(f32[]{:T(128)} %multiply_reduce_fusion.2), channel_id=1, replica_groups=mesh['space'=128,'mode'=4] {'space','mode'}, use_global_device_ids=true, to_apply=%region_1.0 | all-reduce | flops 1 | bytes 8 | tf_op jit(solution)/shard_map/psum | solution.py:96
  111.8 1.9 gather_fusion.2
  117.9 9.6 all-to-all-start
  128.3 3.5 collective-permute-start
  131.9 2.1 collective-permute-start.1
  136.7 8.7 collective-permute-done
  145.6 3.8 collective-permute-done.1
  149.8 4.1 gather_fusion.1
  154.0 2.4 copy.530
  162.2 3.4 dot_general.55
  165.6 5.1 fusion.4
  170.8 4.0 copy.357
  174.8 23.9 %scatter_fusion = f32[33,2,7,64]{3,1,2,0:T(2,128)S(1)} fusion(f32[33,2,7,64]{3,1,2,0:T(2,128)S(1)} %broadcast.411.clone, s32[256]{0:T(256)S(1)} %copy-done.30, f32[256,2,7,64]{3,1,2,0:T(2,128)} %copy.357), kind=kCustom, calls=%fused_computation.10 | custom fusion | flops 229376 | bytes 2753536 | tf_op jit(solution)/shard_map/scatter-add | solution.py:123
  204.2 97.1 %psum.71 = f32[2]{0:T(128)S(1)} all-reduce(f32[2]{0:T(128)S(1)} %pad_maximum_fusion.7), channel_id=1, replica_groups=mesh['space'=128,'mode'=4] {'space','mode'}, use_global_device_ids=true, to_apply=%region_6.0 | all-reduce | flops 2 | bytes 16 | tf_op jit(solution)/shard_map/psum | solution.py:127
  302.4 2.0 fusion.81
  306.9 95.2 %psum.72 = f32[]{:T(128)} all-reduce(f32[]{:T(128)} %multiply_reduce_fusion.1), channel_id=1, replica_groups=mesh['space'=128,'mode'=4] {'space','mode'}, use_global_device_ids=true, to_apply=%region_8.0 | all-reduce | flops 1 | bytes 8 | tf_op jit(solution)/shard_map/psum | solution.py:130
  404.1 2.8 gather_fusion.5
  406.8 1.6 copy.373
  409.5 2.4 scatter_custom_fusion.2
  412.0 2.7 reshape.957
  414.6 11.5 all-to-all-start.1
  428.3 3.5 collective-permute-start.2
  431.8 1.9 collective-permute-start.3
  436.3 6.4 collective-permute-done.2
  442.9 5.2 collective-permute-done.3
  448.4 2.0 gather_fusion.4
  450.4 2.4 copy.532
  458.7 3.4 dot_general.61
  462.1 5.1 fusion.2
  467.3 4.0 copy.377
  471.3 23.9 %scatter_fusion.1 = f32[33,2,7,64]{3,1,2,0:T(2,128)S(1)} fusion(f32[33,2,7,64]{3,1,2,0:T(2,128)S(1)} %broadcast.411.clone.1, s32[256]{0:T(256)S(1)} %copy-done.31, f32[256,2,7,64]{3,1,2,0:T(2,128)} %copy.377), kind=kCustom, calls=%fused_computation.12 | custom fusion | flops 229376 | bytes 2753536 | tf_op jit(solution)/shard_map/scatter-add | solution.py:123
  496.1 1.6 squeeze.68
  499.3 1.6 fusion.56
  503.1 97.1 %psum.73 = f32[2]{0:T(128)S(1)} all-reduce(f32[2]{0:T(128)S(1)} %pad_maximum_fusion.8), channel_id=1, replica_groups=mesh['space'=128,'mode'=4] {'space','mode'}, use_global_device_ids=true, to_apply=%region_13.0 | all-reduce | flops 2 | bytes 16 | tf_op jit(solution)/shard_map/psum | solution.py:127
  601.9 2.3 fusion.77
  606.8 95.3 %psum.74 = f32[2]{0:T(128)S(1)} all-reduce(f32[2]{0:T(128)S(1)} %pad_maximum_fusion.9), channel_id=1, replica_groups=mesh['space'=128,'mode'=4] {'space','mode'}, use_global_device_ids=true, to_apply=%region_16.0 | all-reduce | flops 2 | bytes 16 | tf_op jit(solution)/shard_map/psum | solution.py:127
  702.6 2.8 fusion.79
  709.5 1.6 copy.387
  712.7 1.6 copy.384
  716.9 1.8 multiply_reduce_fusion
  718.7 93.8 %psum.75 = f32[]{:T(128)} all-reduce(f32[]{:T(128)} %multiply_reduce_fusion), channel_id=1, replica_groups=mesh['space'=128,'mode'=4] {'space','mode'}, use_global_device_ids=true, to_apply=%region_18.0 | all-reduce | flops 1 | bytes 8 | tf_op jit(solution)/shard_map/psum | solution.py:130
  816.0 4.7 collective-permute-start.4
  820.7 1.9 collective-permute-start.5
  822.7 2.9 gather_fusion.8
  825.6 2.0 copy.395
  828.7 2.4 scatter_custom_fusion.4
  831.2 2.7 reshape.964
  833.8 12.3 all-to-all-start.2
  850.9 2.0 gather_fusion.7
  853.0 2.4 copy.531
  861.3 13.0 all-to-all-done.2
  874.2 3.4 dot_general.67
  877.6 5.1 fusion
  882.8 3.1 copy.399
  886.0 15.5 %scatter_fusion.2 = f32[33,2,7,64]{3,1,2,0:T(2,128)S(1)} fusion(f32[33,2,7,64]{3,1,2,0:T(2,128)S(1)} %broadcast.411, s32[256]{0:T(256)S(1)} %copy-done.31, f32[256,2,7,64]{3,1,2,0:T(2,128)S(1)} %copy.399), kind=kCustom, calls=%fused_computation.14 | custom fusion | flops 229376 | bytes 2753536 | tf_op jit(solution)/shard_map/scatter-add | solution.py:123
  904.5 95.0 %psum.76 = f32[2]{0:T(128)S(1)} all-reduce(f32[2]{0:T(128)S(1)} %pad_maximum_fusion.10), channel_id=1, replica_groups=mesh['space'=128,'mode'=4] {'space','mode'}, use_global_device_ids=true, to_apply=%region_23.0 | all-reduce | flops 2 | bytes 16 | tf_op jit(solution)/shard_map/psum | solution.py:127
  1000.3 1.7 fusion.75
  1004.6 93.6 %psum.77 = f32[2]{0:T(128)S(1)} all-reduce(f32[2]{0:T(128)S(1)} %pad_maximum_fusion.11), channel_id=1, replica_groups=mesh['space'=128,'mode'=4] {'space','mode'}, use_global_device_ids=true, to_apply=%region_26.0 | all-reduce | flops 2 | bytes 16 | tf_op jit(solution)/shard_map/psum | solution.py:127
  1098.9 1.7 fusion.73
  1103.3 95.3 %psum.78 = f32[2]{0:T(128)S(1)} all-reduce(f32[2]{0:T(128)S(1)} %pad_maximum_fusion.12), channel_id=1, replica_groups=mesh['space'=128,'mode'=4] {'space','mode'}, use_global_device_ids=true, to_apply=%region_29.0 | all-reduce | flops 2 | bytes 16 | tf_op jit(solution)/shard_map/psum | solution.py:127
  1199.3 1.7 fusion.71
  1202.0 1.9 broadcast_select_fusion
  1206.0 94.6 %psum.79 = f32[]{:T(128)} all-reduce(f32[]{:T(128)} %fusion.43), channel_id=1, replica_groups=mesh['space'=128,'mode'=4] {'space','mode'}, use_global_device_ids=true, to_apply=%region_31.0 | all-reduce | flops 1 | bytes 8 | tf_op jit(solution)/shard_map/psum | solution.py:130
  (285 shorter events, 87.4 us)
Async XLA Ops:
  0.6 165.0 %copy-start = (f32[64,64]{1,0:T(8,128)S(1)}, f32[64,64]{1,0:T(8,128)}, u32[]{:S(2)}) copy-start(f32[64,64]{1,0:T(8,128)} %param.35) | copy-start | bytes 49156
  110.1 0.7 copy-start.5
  111.0 3.7 copy-start.40
  111.8 292.2 %copy-start.37 = (s32[1024]{0:T(1024)}, s32[1024]{0:T(1024)S(1)}, u32[]{:S(2)}) copy-start(s32[1024]{0:T(1024)S(1)} %pad_clamp_fusion) | copy-start | bytes 12292
  113.8 1.3 copy-start.42
  114.8 293.7 %copy-start.32 = (f32[128]{0:T(128)}, f32[128]{0:T(128)S(1)}, u32[]{:S(2)}) copy-start(f32[128]{0:T(128)S(1)} %get-tuple-element.218) | copy-start | bytes 1540
  114.8 293.7 %copy-start.34 = (f32[128]{0:T(128)}, f32[128]{0:T(128)S(1)}, u32[]{:S(2)}) copy-start(f32[128]{0:T(128)S(1)} %get-tuple-element.219) | copy-start | bytes 1540
  115.1 294.4 %copy-start.44 = (s32[128]{0:T(128)}, s32[128]{0:T(128)S(1)}, u32[]{:S(2)}) copy-start(s32[128]{0:T(128)S(1)} %compare_select_fusion.2) | copy-start | bytes 1540
  116.4 11.1 copy-start.43
  116.4 17.6 %copy-start.38 = (s32[6,32]{1,0:T(8,128)S(1)}, s32[6,32]{1,0:T(8,128)}, u32[]{:S(2)}) copy-start(s32[6,32]{1,0:T(8,128)} %param.29) | copy-start | bytes 2308
  116.4 17.7 %copy-start.25 = (f32[2,7,7,7,32]{4,0,3,2,1:T(2,128)S(1)}, f32[2,7,7,7,32]{4,0,3,2,1:T(2,128)}, u32[]{:S(2)}) copy-start(f32[2,7,7,7,32]{4,0,3,2,1:T(2,128)} %param.28) | copy-start | bytes 263428
  117.9 44.3 %all-to-all-start = ((f32[128,2,896]{2,1,0:T(2,128)}), f32[128,2,896]{2,1,0:T(2,128)}, u32[]{:S(2)}, u32[]{:S(2)}) async-start(f32[128,2,896]{2,1,0:T(2,128)} %reshape.950), calls=%async_computation | async-start | bytes 1835008 | tf_op jit(solution)/shard_map/all_to_all | solution.py:113
  127.5 300.1 %copy-start.36 = (s32[1024]{0:T(1024)}, s32[1024]{0:T(1024)S(1)}, u32[]{:S(2)}) copy-start(s32[1024]{0:T(1024)S(1)} %pad_clamp_fusion.2) | copy-start | bytes 12292
  128.3 17.1 %collective-permute-start = (f32[2,7,1024]{2,0,1:T(2,128)S(1)}, f32[2,7,1024]{2,0,1:T(2,128)S(1)}, u32[]{:S(2)}, u32[]{:S(2)}) collective-permute-start(f32[2,7,1024]{2,0,1:T(2,128)S(1)} %reshape.946), channel_id=1, source_target_pairs={{0,4},{4,8},{8,12},{12,16},{16,20},{20,24},{24,28},{28,32},{32,36}... | collective-permute-start | bytes 172040 | tf_op jit(solution)/shard_map/ppermute | solution.py:26
  131.9 17.5 %collective-permute-start.1 = (f32[2,7,1024]{2,0,1:T(2,128)S(1)}, f32[2,7,1024]{2,0,1:T(2,128)S(1)}, u32[]{:S(2)}, u32[]{:S(2)}) collective-permute-start(f32[2,7,1024]{2,0,1:T(2,128)S(1)} %reshape.946), channel_id=1, source_target_pairs={{4,0},{8,4},{12,8},{16,12},{20,16},{24,20},{28,24},{32,28},{36,32}... | collective-permute-start | bytes 172040 | tf_op jit(solution)/shard_map/ppermute | solution.py:29
  135.6 66.5 %copy-start.9 = (f32[1,1,7,2048]{3,0,2,1:T(1,128)}, f32[1,1,7,2048]{3,0,2,1:T(1,128)S(1)}, u32[]{:S(2)}) copy-start(f32[1,1,7,2048]{3,0,2,1:T(1,128)S(1)} %get-tuple-element.190) | copy-start | bytes 172036
  135.7 66.5 %copy-start.12 = (f32[1,1,7,2048]{3,0,2,1:T(1,128)}, f32[1,1,7,2048]{3,0,2,1:T(1,128)S(1)}, u32[]{:S(2)}) copy-start(f32[1,1,7,2048]{3,0,2,1:T(1,128)S(1)} %get-tuple-element.191) | copy-start | bytes 172036
  136.0 170.2 %copy-start.1 = (f32[1,7,32,64]{3,1,2,0:T(8,128)}, f32[1,7,32,64]{3,1,2,0:T(8,128)S(1)}, u32[]{:S(2)}) copy-start(f32[1,7,32,64]{3,1,2,0:T(8,128)S(1)} %copy.351) | copy-start | bytes 172036
  136.7 17.3 %copy-start.26 = (s32[1024]{0:T(1024)}, s32[1024]{0:T(1024)S(1)}, u32[]{:S(2)}) copy-start(s32[1024]{0:T(1024)S(1)} %pad_clamp_fusion.1) | copy-start | bytes 12292
  170.8 4.1 copy-start.30
  306.2 96.5 %copy-start.3 = (f32[1,7,32,64]{3,1,2,0:T(8,128)}, f32[1,7,32,64]{3,1,2,0:T(8,128)S(1)}, u32[]{:S(2)}) copy-start(f32[1,7,32,64]{3,1,2,0:T(8,128)S(1)} %copy.364) | copy-start | bytes 172036
  412.0 14.8 %copy-start.41 = (s32[3]{0:T(128)S(1)}, s32[3]{0:T(128)}, u32[]{:S(2)}) copy-start(s32[3]{0:T(128)} %constant.302.clone.1) | copy-start | bytes 40
  414.6 19.3 %copy-start.19 = (f32[1,1,7,2048]{3,0,2,1:T(1,128)S(1)}, f32[1,1,7,2048]{3,0,2,1:T(1,128)}, u32[]{:S(2)}) copy-start(f32[1,1,7,2048]{3,0,2,1:T(1,128)} %get-tuple-element.189) | copy-start | bytes 172036
  414.6 44.1 %all-to-all-start.1 = ((f32[128,2,896]{2,1,0:T(2,128)}), f32[128,2,896]{2,1,0:T(2,128)}, u32[]{:S(2)}, u32[]{:S(2)}) async-start(f32[128,2,896]{2,1,0:T(2,128)} %reshape.957), calls=%async_computation.1 | async-start | bytes 1835008 | tf_op jit(solution)/shard_map/all_to_all | solution.py:113
  428.3 14.5 %collective-permute-start.2 = (f32[2,7,1024]{2,0,1:T(2,128)S(1)}, f32[2,7,1024]{2,0,1:T(2,128)S(1)}, u32[]{:S(2)}, u32[]{:S(2)}) collective-permute-start(f32[2,7,1024]{2,0,1:T(2,128)S(1)} %reshape.952), channel_id=1, source_target_pairs={{0,4},{4,8},{8,12},{12,16},{16,20},{20,24},{24,28},{28,32},{32,36}... | collective-permute-start | bytes 172040 | tf_op jit(solution)/shard_map/ppermute | solution.py:26
  431.8 16.3 %collective-permute-start.3 = (f32[2,7,1024]{2,0,1:T(2,128)S(1)}, f32[2,7,1024]{2,0,1:T(2,128)S(1)}, u32[]{:S(2)}, u32[]{:S(2)}) collective-permute-start(f32[2,7,1024]{2,0,1:T(2,128)S(1)} %reshape.952), channel_id=1, source_target_pairs={{4,0},{8,4},{12,8},{16,12},{20,16},{24,20},{28,24},{32,28},{36,32}... | collective-permute-start | bytes 172040 | tf_op jit(solution)/shard_map/ppermute | solution.py:29
  434.7 13.7 %copy-start.27 = (s32[1024]{0:T(1024)S(1)}, s32[1024]{0:T(1024)}, u32[]{:S(2)}) copy-start(s32[1024]{0:T(1024)} %copy-done.26) | copy-start | bytes 12292
  436.3 280.6 %copy-start.2 = (f32[1,7,32,64]{3,1,2,0:T(8,128)}, f32[1,7,32,64]{3,1,2,0:T(8,128)S(1)}, u32[]{:S(2)}) copy-start(f32[1,7,32,64]{3,1,2,0:T(8,128)S(1)} %copy.371) | copy-start | bytes 172036
  467.3 4.1 copy-start.31
  495.2 4.1 copy-start.10
  495.3 4.1 copy-start.13
  495.4 111.4 %copy-start.39 = (f32[2,1,1]{0,2,1:T(1,128)S(1)}, f32[2,1,1]{0,2,1:T(1,128)}, u32[]{:S(2)}) copy-start(f32[2,1,1]{0,2,1:T(1,128)} %get-tuple-element.204) | copy-start | bytes 28
  601.9 103.6 %copy-start.7 = (f32[2,7,2048]{2,0,1:T(2,128)}, f32[2,7,2048]{2,0,1:T(2,128)S(1)}, u32[]{:S(2)}) copy-start(f32[2,7,2048]{2,0,1:T(2,128)S(1)} %reshape.959) | copy-start | bytes 344068
  604.2 101.2 %copy-start.17 = (f32[1,1,7,2048]{3,0,2,1:T(1,128)}, f32[1,1,7,2048]{3,0,2,1:T(1,128)S(1)}, u32[]{:S(2)}) copy-start(f32[1,1,7,2048]{3,0,2,1:T(1,128)S(1)} %get-tuple-element.187) | copy-start | bytes 172036
  604.2 114.4 %copy-start.15 = (f32[1,1,7,2048]{3,0,2,1:T(1,128)}, f32[1,1,7,2048]{3,0,2,1:T(1,128)S(1)}, u32[]{:S(2)}) copy-start(f32[1,1,7,2048]{3,0,2,1:T(1,128)S(1)} %get-tuple-element.153) | copy-start | bytes 172036
  716.9 1.8 copy-start.4
  816.0 11.6 copy-start.33
  816.0 11.6 copy-start.35
  816.0 33.6 %collective-permute-start.4 = (f32[2,7,1024]{2,0,1:T(2,128)}, f32[2,7,1024]{2,0,1:T(2,128)S(1)}, u32[]{:S(2)}, u32[]{:S(2)}) collective-permute-start(f32[2,7,1024]{2,0,1:T(2,128)} %reshape.960), channel_id=1, source_target_pairs={{0,4},{4,8},{8,12},{12,16},{16,20},{20,24},{24,28},{28,32},{32,36}... | collective-permute-start | bytes 172040 | tf_op jit(solution)/shard_map/ppermute | solution.py:26
  820.7 29.1 %collective-permute-start.5 = (f32[2,7,1024]{2,0,1:T(2,128)}, f32[2,7,1024]{2,0,1:T(2,128)}, u32[]{:S(2)}, u32[]{:S(2)}) collective-permute-start(f32[2,7,1024]{2,0,1:T(2,128)} %reshape.960), channel_id=1, source_target_pairs={{4,0},{8,4},{12,8},{16,12},{20,16},{24,20},{28,24},{32,28},{36,32}... | collective-permute-start | bytes 172040 | tf_op jit(solution)/shard_map/ppermute | solution.py:29
  831.1 15.2 %copy-start.8 = (f32[2,7,2048]{2,0,1:T(2,128)S(1)}, f32[2,7,2048]{2,0,1:T(2,128)}, u32[]{:S(2)}) copy-start(f32[2,7,2048]{2,0,1:T(2,128)} %copy-done.7) | copy-start | bytes 344068
  831.2 15.2 %copy-start.16 = (f32[1,1,7,2048]{3,0,2,1:T(1,128)S(1)}, f32[1,1,7,2048]{3,0,2,1:T(1,128)}, u32[]{:S(2)}) copy-start(f32[1,1,7,2048]{3,0,2,1:T(1,128)} %copy-done.15) | copy-start | bytes 172036
  831.2 15.2 %copy-start.18 = (f32[1,1,7,2048]{3,0,2,1:T(1,128)S(1)}, f32[1,1,7,2048]{3,0,2,1:T(1,128)}, u32[]{:S(2)}) copy-start(f32[1,1,7,2048]{3,0,2,1:T(1,128)} %copy-done.17) | copy-start | bytes 172036
  831.2 15.2 %copy-start.20 = (f32[1,7,2048]{2,0,1:T(1,128)S(1)}, f32[1,7,2048]{2,0,1:T(1,128)}, u32[]{:S(2)}) copy-start(f32[1,7,2048]{2,0,1:T(1,128)} %get-tuple-element.157) | copy-start | bytes 172036
  831.2 15.2 %copy-start.21 = (f32[1,7,2048]{2,0,1:T(1,128)S(1)}, f32[1,7,2048]{2,0,1:T(1,128)}, u32[]{:S(2)}) copy-start(f32[1,7,2048]{2,0,1:T(1,128)} %get-tuple-element.185) | copy-start | bytes 172036
  833.8 40.4 %all-to-all-start.2 = ((f32[128,2,896]{2,1,0:T(2,128)}), f32[128,2,896]{2,1,0:T(2,128)}, u32[]{:S(2)}, u32[]{:S(2)}) async-start(f32[128,2,896]{2,1,0:T(2,128)} %reshape.964), calls=%async_computation.2 | async-start | bytes 1835008 | tf_op jit(solution)/shard_map/all_to_all | solution.py:113
  849.6 1.2 copy-start.28
  901.4 0.8 copy-start.11
  901.5 0.8 copy-start.14
  901.6 103.0 %copy-start.29 = (f32[2,4,3]{0,2,1:T(4,128)S(1)}, f32[2,4,3]{0,2,1:T(4,128)}, u32[]{:S(2)}) copy-start(f32[2,4,3]{0,2,1:T(4,128)} %copy-done.28) | copy-start | bytes 292
  1201.5 101.0 %copy-start.23 = (f32[1,2,7,2048]{3,0,2,1:T(1,128)S(1)}, f32[1,2,7,2048]{3,0,2,1:T(1,128)}, u32[]{:S(2)}) copy-start(f32[1,2,7,2048]{3,0,2,1:T(1,128)} %pad_maximum_fusion.6) | copy-start | bytes 344068
  1201.5 101.0 %copy-start.24 = (f32[1,2,7,2048]{3,1,2,0:T(2,128)S(1)}, f32[1,2,7,2048]{3,1,2,0:T(2,128)}, u32[]{:S(2)}) copy-start(f32[1,2,7,2048]{3,1,2,0:T(2,128)} %reshape.951) | copy-start | bytes 344068
  1201.7 101.0 %copy-start.6 = (f32[1,2,7,2048]{3,1,2,0:T(2,128)S(1)}, f32[1,2,7,2048]{3,1,2,0:T(2,128)}, u32[]{:S(2)}) copy-start(f32[1,2,7,2048]{3,1,2,0:T(2,128)} %copy-done.5) | copy-start | bytes 344068
  1201.7 101.0 %copy-start.22 = (f32[1,2,7,2048]{3,1,2,0:T(2,128)S(1)}, f32[1,2,7,2048]{3,1,2,0:T(2,128)}, u32[]{:S(2)}) copy-start(f32[1,2,7,2048]{3,1,2,0:T(2,128)} %copy.415) | copy-start | bytes 344068
where the time goes:
time: 1310 us; the launch traced here: 1300 us
  blocking collectives  963 us (74%)
  local copies, waits for them, and re-layouts  108 us (8%)
  other arithmetic  107 us (8%)
  starting transfers between devices  51.1 us (4%)
  waiting for transfers between devices  37.1 us (3%)
  matrix products  33 us (3%)
    psum x6, blocking collectives, local(): lax.psum(local_inner(vectors[index], image), ('space', 'mode')) / count  573 us
    psum x3, blocking collectives, local(): lax.psum(jnp.sum(image * image), ('space', 'mode')) / count + EPS  284 us
    psum x1, blocking collectives, local(): lax.psum(jnp.sum(forcing * forcing), ('space', 'mode')) / count + EPS  106 us
    scatter-add x3, other arithmetic, local(): jax.ops.segment_sum(arrived, recv_target, num_segments=nblk + 1)[:nblk]  63.2 us
    all_to_all x3, starting transfers between devices, local(): lax.all_to_all(buffer, 'space', split_axis=0, concat_axis=0, tiled=True)  33.4 us
  transfers between devices with their start and end apart: 9, of which 5 were waited for; matrix products, arithmetic and copies ran while one was open for 4% of the time, Pallas kernels for 0%

commit v1 on v0

v1 whole, which is shorter than its diff:
```python
import functools
import math

import jax
import jax.numpy as jnp
from jax import lax
from jax.experimental import pallas as pl
from jax.experimental.pallas import tpu as pltpu
from jax.sharding import PartitionSpec as P

MESH = pl.DeviceIdType.MESH
F32 = jnp.float32
BF16 = jnp.bfloat16
FIELDS = 7
BLK = 64
HB = 16
KRY = 3
NPHASE = 36
NBLK = 32
LANES = 128
SHIFT = 2.0
OMEGA = 0.5
EPS = 1e-06
CHUNKS = 4
STRIDE = 51
ROW = 16


def iota(shape, dim):
    return lax.broadcasted_iota(jnp.int32, shape, dim)


def split(x):
    hi = x.astype(BF16)
    return hi, (x - hi.astype(F32)).astype(BF16)


def matmul(a, b):
    return lax.dot_general(a, b, (((1,), (0,)), ((), ())), preferred_element_type=F32)


def matmul_nt(a, b):
    return lax.dot_general(a, b, (((1,), (1,)), ((), ())), preferred_element_type=F32)


def one_hot(mask):
    return jnp.where(mask, 1.0, 0.0)


def wide(x):
    return jnp.concatenate([x[k] for k in range(FIELDS)], axis=1)


def turn(x, sign):
    return pltpu.roll(x, BLK, axis=x.ndim - 1) * sign


def kernel(
    space,
    modes,
    field_ref,
    jac_ref,
    cols_ref,
    halo_ref,
    blocks_ref,
    slot_ref,
    target_ref,
    phase_ref,
    mortar_ref,
    out_ref,
    hess_ref,
    sbuf,
    rbuf,
    hsend,
    hrecv,
    first_buf,
    second_buf,
    coef,
    pmat,
    tmat,
    nmat,
    hmat,
    bdiag,
    image,
    a2a_send,
    a2a_recv,
    halo_send,
    halo_recv,
    red_send,
    red_recv,
):
    me = lax.axis_index("space")
    mode = lax.axis_index("mode")
    line = 16
    lines = space // line
    wide_group = lines * modes
    in_line = lax.rem(me, line)
    my_line = me // line
    in_wide = my_line * modes + mode
    chunk = space // CHUNKS
    count = float(space * modes * NBLK * BLK)

    def partner(i):
        return lax.rem(me + lax.rem(i * STRIDE, space), space)

    def line_partner(o):
        return {"space": my_line * line + lax.rem(in_line + o, line)}

    def wide_partner(o):
        there = lax.rem(in_wide + o, wide_group)
        return {"space": there // modes * line + in_line, "mode": lax.rem(there, modes)}

    barrier = pltpu.get_barrier_semaphore()

    def greet(i, c):
        pl.semaphore_signal(barrier, inc=1, device_id={"space": partner(i)}, device_id_type=MESH)
        return c

    def greet_wide(o, c):
        pl.semaphore_signal(barrier, inc=1, device_id=wide_partner(o), device_id_type=MESH)
        return c

    lax.fori_loop(1, space, greet, 0)
    lax.fori_loop(1, wide_group, greet_wide, 0)

    lane = iota((1, LANES), 1)
    sign = jnp.where(lane < BLK, -1.0, 1.0).astype(F32)
    level = (mode + 1).astype(F32)

    angle = phase_ref[...].astype(F32) * (level * (2.0 * math.pi / NPHASE))
    picked = one_hot(iota((NBLK, LANES), 0) == blocks_ref[...])
    turned = jnp.concatenate([picked * jnp.cos(angle), picked * jnp.sin(angle)], axis=0)
    t_hi, t_lo = split(turned)
    for c in range(CHUNKS):
        row = iota((2 * chunk, 1), 0)
        reader = partner(c * chunk + lax.rem(row, chunk))
        chosen = one_hot(slot_ref[...] == reader * 2 + row // chunk).astype(BF16)
        p_hi = matmul_nt(chosen, t_hi).astype(BF16)
        p_lo = matmul_nt(chosen, t_lo).astype(BF16)
        pmat[c] = jnp.concatenate([p_hi, p_lo, p_hi], axis=1)
    eye = one_hot(iota((NBLK, NBLK), 0) == iota((NBLK, NBLK), 1)).astype(BF16)
    halo_t = one_hot(iota((NBLK, HB), 0) == halo_ref[...]).astype(BF16)
    eye_h = one_hot(iota((HB, HB), 0) == iota((HB, HB), 1)).astype(BF16)
    picks = matmul_nt(eye_h, halo_t).astype(BF16)
    hmat[...] = jnp.concatenate([picks, picks], axis=1)

    for t in range(KRY):
        rbuf[t, 0] = jnp.zeros((ROW, LANES), F32)

    pl.semaphore_wait(barrier, space - 1 + wide_group - 1)

    def send_halo(t, hi, lo):
        packed = matmul(hmat[...], jnp.concatenate([hi, lo], axis=0))
        for k in range(FIELDS):
            hsend[t, k] = packed[:, k * LANES : (k + 1) * LANES]
        for side in range(2):
            there = lax.rem(me + (1 if side == 0 else space - 1), space)
            pltpu.make_async_remote_copy(
                hsend.at[t],
                hrecv.at[t, side],
                halo_send.at[t, side],
                halo_recv.at[t, side],
                device_id={"space": there},
                device_id_type=MESH,
            ).start()

    def halo_copy(t, side, sem):
        return pltpu.make_async_copy(hsend.at[t], hrecv.at[t, side], sem.at[t, side])

    def send_chunk(t, c, rows):
        packed = matmul(pmat[c], rows)
        flat = sbuf.at[t].reshape(space * ROW, LANES)
        for slot in range(2):
            for k in range(FIELDS):
                flat[pl.ds(c * chunk * ROW + slot * FIELDS + k, chunk, stride=ROW), :] = packed[
                    slot * chunk : (slot + 1) * chunk, k * LANES : (k + 1) * LANES
                ]

        def one(i, carry):
            pltpu.make_async_remote_copy(
                sbuf.at[t, i, pl.ds(0, 2 * FIELDS)],
                rbuf.at[t, i, pl.ds(0, 2 * FIELDS)],
                a2a_send.at[t, c],
                a2a_recv.at[t, c],
                device_id={"space": partner(i)},
                device_id_type=MESH,
            ).start()
            return carry

        lax.fori_loop(1 if c == 0 else c * chunk, (c + 1) * chunk, one, 0)

    def wait_chunk(t, c, sem):
        number = chunk - 1 if c == 0 else chunk
        part = rbuf.at[t, pl.ds(0, number), pl.ds(0, 2 * FIELDS)]
        pltpu.make_async_copy(part, part, sem.at[t, c]).wait()

    def start_sum(r, values):
        vector = jnp.zeros((1, LANES), F32)
        for n, value in enumerate(values):
            vector = jnp.where(lane == n, value, vector)
        first_buf[r, in_line] = vector

        def one(o, carry):
            pltpu.make_async_remote_copy(
                first_buf.at[r, in_line],
                first_buf.at[r, in_line],
                red_send.at[r, 0],
                red_recv.at[r, 0],
                device_id=line_partner(o),
                device_id_type=MESH,
            ).start()
            return carry

        lax.fori_loop(1, line, one, 0)

    def middle_sum(r):
        part = first_buf.at[r, pl.ds(0, line - 1)]
        pltpu.make_async_copy(part, part, red_recv.at[r, 0]).wait()
        second_buf[r, in_wide] = jnp.sum(first_buf[r], axis=0)

        def one(o, carry):
            pltpu.make_async_remote_copy(
                second_buf.at[r, in_wide],
                second_buf.at[r, in_wide],
                red_send.at[r, 1],
                red_recv.at[r, 1],
                device_id=wide_partner(o),
                device_id_type=MESH,
            ).start()
            return carry

        lax.fori_loop(1, wide_group, one, 0)

    def end_sum(r, number):
        part = second_buf.at[r, pl.ds(0, wide_group - 1)]
        pltpu.make_async_copy(part, part, red_recv.at[r, 1]).wait()
        total = jnp.sum(second_buf[r], axis=0) * (1.0 / count)
        return [
            jnp.sum(jnp.where(lane == n, total, 0.0), axis=1, keepdims=True) for n in range(number)
        ]

    def total(x):
        return jnp.sum(jnp.sum(jnp.sum(x, axis=0), axis=0, keepdims=True), axis=1, keepdims=True)

    def inner(left, right):
        return [total(left * right), total(turn(left, sign) * right)]

    def minus(field, factor, vector):
        return field - factor[0] * vector - factor[1] * turn(vector, sign)

    def prepare():
        ones = jnp.ones((1, LANES), F32)
        for h in range(2):
            part = jac_ref[:, h, :]
            hi = part.astype(BF16)
            mid = (part - hi.astype(F32)).astype(BF16)
            low = (part - hi.astype(F32) - mid.astype(F32)).astype(BF16)
            columns = matmul_nt(eye, hi) + matmul_nt(eye, mid) + matmul_nt(eye, low)
            for o in range(FIELDS):
                for i in range(FIELDS):
                    for j in range(FIELDS):
                        q = (o * FIELDS + i) * FIELDS + j
                        value = columns[:, q : q + 1]
                        if j == 0 and o == i:
                            value = value + (SHIFT if h == 0 else OMEGA * level)
                        coef[q, h] = value * (ones if h == 0 else sign)
        for j in range(FIELDS - 1):
            source = one_hot(iota((2 * NBLK, NBLK), 0) == cols_ref[j : j + 1, :]).astype(BF16)
            there = matmul_nt(eye, source).astype(BF16)
            nmat[j * NBLK : (j + 1) * NBLK, :] = jnp.concatenate([there, there], axis=1)
        block = one_hot(iota((NBLK, 2 * space), 0) == target_ref[...]).astype(BF16)
        for c in range(CHUNKS):
            row = iota((2 * chunk, 1), 0)
            index = lax.rem((c * chunk + lax.rem(row, chunk)) * STRIDE, space)
            writer = lax.rem(me + space - index, space)
            pick = one_hot(iota((2 * chunk, 2 * space), 1) == writer * 2 + row // chunk)
            there = matmul_nt(block, pick.astype(BF16)).astype(BF16)
            tmat[c] = jnp.concatenate([there, there], axis=1)
        bdiag[...] = jnp.zeros((LANES, LANES), F32)
        bdiag[0:BLK, 0:BLK] = mortar_ref[...]
        bdiag[BLK:LANES, BLK:LANES] = mortar_ref[...]

    def flux(t, field, hi, lo):
        sides = []
        for side in range(2):
            halo_copy(t, side, halo_recv).wait()
            there = wide(hrecv[t, side])
            edge = (me > 0) if side == 0 else (me < space - 1)
            sides.append(split(jnp.where(edge, there, 0.0)))
        sources = jnp.concatenate(
            [hi, sides[0][0], sides[1][0], lo, sides[0][1], sides[1][1]], axis=0
        )
        gathered = matmul(nmat[...], sources)
        for k in range(FIELDS):
            image[0, k] = field[k]
            for j in range(FIELDS - 1):
                image[j + 1, k] = gathered[j * NBLK : (j + 1) * NBLK, k * LANES : (k + 1) * LANES]

        def one(n, totals):
            j = n // FIELDS
            i = lax.rem(n, FIELDS)
            value = image[j, i]
            other = pltpu.roll(value, BLK, axis=1)
            return tuple(
                totals[o]
                + coef[o * FIELDS * FIELDS + i * FIELDS + j, 0] * value
                + coef[o * FIELDS * FIELDS + i * FIELDS + j, 1] * other
                for o in range(FIELDS)
            )

        zero = jnp.zeros((NBLK, LANES), F32)
        return lax.fori_loop(0, FIELDS * FIELDS, one, (zero,) * FIELDS)

    def arrived(t):
        sums = jnp.zeros((NBLK, FIELDS * LANES), F32)
        flat = rbuf.at[t].reshape(space * ROW, LANES)
        for c in range(CHUNKS):
            wait_chunk(t, c, a2a_recv)
            rows = jnp.concatenate(
                [
                    jnp.concatenate(
                        [
                            flat[
                                pl.ds(c * chunk * ROW + slot * FIELDS + k, chunk, stride=ROW), :
                            ]
                            for k in range(FIELDS)
                        ],
                        axis=1,
                    )
                    for slot in range(2)
                ],
                axis=0,
            )
            hi, lo = split(rows)
            sums = sums + matmul(tmat[c], jnp.concatenate([hi, lo], axis=0))
        rows = jnp.concatenate(
            [sums[:, k * LANES : (k + 1) * LANES] for k in range(FIELDS)], axis=0
        )
        hi, lo = split(rows)
        m_hi, m_lo = split(bdiag[...])
        return matmul(hi, m_hi) + (matmul(lo, m_hi) + matmul(hi, m_lo))

    def step(t, field, reduce_ops):
        flatly = wide(field)
        hi, lo = split(flatly)
        send_halo(t, hi, lo)
        reduce_ops[0]()
        i_hi, i_lo = split(wide(turn(field, sign)))
        rows = jnp.concatenate([hi, i_hi, hi, i_hi, lo, i_lo], axis=0)
        for c in range(CHUNKS):
            send_chunk(t, c, rows)
            if c + 1 < len(reduce_ops):
                reduce_ops[c + 1]()
        if t == 0:
            prepare()
        totals = flux(t, field, hi, lo)
        mortared = arrived(t)
        return jnp.stack(
            [totals[k] + mortared[k * NBLK : (k + 1) * NBLK] for k in range(FIELDS)]
        )

    hess = []
    forcing = field_ref[...]
    state = {}

    def end_first():
        state["first"] = jnp.sqrt(end_sum(0, 1)[0] + EPS)

    image0 = step(
        0,
        forcing,
        [
            lambda: start_sum(0, [total(forcing * forcing)]),
            lambda: middle_sum(0),
            lambda: None,
            end_first,
        ],
    )
    first = state["first"]
    out_ref[0] = forcing / first
    images = [jnp.where(first < jnp.inf, image0 / first, 0.0)]
    vectors = 1

    for t in range(1, KRY + 1):
        w = images[t - 1]

        def start_products(t=t, w=w):
            products = []
            for index in range(t):
                products += inner(out_ref[index], w)
            start_sum(2 * t - 1, products)

        def end_products(t=t, w=w):
            values = end_sum(2 * t - 1, 2 * t)
            factors = [(values[2 * n], values[2 * n + 1]) for n in range(t)]
            rest = w
            for index in range(t):
                rest = minus(rest, factors[index], out_ref[index])
            out_ref[t] = rest
            state["factors"] = factors
            start_sum(2 * t, [total(rest * rest)])

        def end_norm(t=t):
            length = jnp.sqrt(end_sum(2 * t, 1)[0] + EPS)
            state["length"] = length
            out_ref[t] = out_ref[t] / length

        middle = [
            lambda t=t: middle_sum(2 * t - 1),
            end_products,
            lambda t=t: middle_sum(2 * t),
        ]
        if t < KRY:
            plain = step(t, w, [start_products] + middle + [end_norm])
        else:
            for op in [start_products] + middle + [end_norm]:
                op()
        factors, length = state["factors"], state["length"]
        hess.append((factors, length))
        if t < KRY:
            for index in range(t):
                plain = minus(plain, factors[index], images[index])
            images.append(plain / length)

    row = iota((8, LANES), 0)
    column = iota((8, LANES), 1)
    table = jnp.zeros((8, LANES), F32)
    for j, (factors, length) in enumerate(hess):
        for index, factor in enumerate(factors):
            for part in range(2):
                table = jnp.where((row == part * 4 + index) & (column == j), factor[part], table)
        table = jnp.where((row == j + 1) & (column == j), length, table)
    hess_ref[...] = table

    for t in range(KRY):
        for side in range(2):
            halo_copy(t, side, halo_send).wait()
        for c in range(CHUNKS):
            wait_chunk(t, c, a2a_send)
    for r in range(2 * KRY + 1):
        part = first_buf.at[r, pl.ds(0, line - 1)]
        pltpu.make_async_copy(part, part, red_send.at[r, 0]).wait()
        part = second_buf.at[r, pl.ds(0, wide_group - 1)]
        pltpu.make_async_copy(part, part, red_send.at[r, 1]).wait()


def solution(mesh):
    space, modes = mesh.shape["space"], mesh.shape["mode"]
    wide_group = space // 16 * modes
    sums = 2 * KRY + 1
    dma = pltpu.SemaphoreType.DMA

    def local(right, jac, cols, halo, blocks, slot, target, phase, mortar):
        field = right[0].reshape(2, FIELDS, NBLK, BLK).transpose(1, 2, 0, 3)
        field = field.reshape(FIELDS, NBLK, LANES)
        jac = jac.transpose(1, 2, 3, 0, 4).reshape(FIELDS**3, 2, NBLK)
        vmem = pl.BlockSpec(memory_space=pltpu.VMEM)
        basis, table = pl.pallas_call(
            functools.partial(kernel, space, modes),
            out_shape=(
                jax.ShapeDtypeStruct((KRY + 1, FIELDS, NBLK, LANES), F32),
                jax.ShapeDtypeStruct((8, LANES), F32),
            ),
            in_specs=[vmem] * 9,
            out_specs=(vmem, vmem),
            scratch_shapes=[
                pltpu.VMEM((KRY, space, ROW, LANES), F32),
                pltpu.VMEM((KRY, space, ROW, LANES), F32),
                pltpu.VMEM((KRY, FIELDS, HB, LANES), F32),
                pltpu.VMEM((KRY, 2, FIELDS, HB, LANES), F32),
                pltpu.VMEM((sums, 16, 1, LANES), F32),
                pltpu.VMEM((sums, wide_group, 1, LANES), F32),
                pltpu.VMEM((FIELDS**3, 2, NBLK, LANES), F32),
                pltpu.VMEM((CHUNKS, 2 * space // CHUNKS, 6 * NBLK), BF16),
                pltpu.VMEM((CHUNKS, NBLK, 4 * space // CHUNKS), BF16),
                pltpu.VMEM(((FIELDS - 1) * NBLK, 4 * NBLK), BF16),
                pltpu.VMEM((HB, 2 * NBLK), BF16),
                pltpu.VMEM((LANES, LANES), F32),
                pltpu.VMEM((FIELDS, FIELDS, NBLK, LANES), F32),
                dma((KRY, CHUNKS)),
                dma((KRY, CHUNKS)),
                dma((KRY, 2)),
                dma((KRY, 2)),
                dma((sums, 2)),
                dma((sums, 2)),
            ],
            compiler_params=pltpu.CompilerParams(
                collective_id=0, has_side_effects=True, vmem_limit_bytes=48 << 20
            ),
        )(
            field,
            jac,
            cols,
            halo.reshape(1, HB),
            blocks.reshape(1, LANES),
            slot.reshape(1, LANES),
            target.reshape(1, 2 * space),
            phase,
            mortar,
        )
        basis = basis.reshape(KRY + 1, FIELDS, NBLK, 2, BLK).transpose(0, 3, 1, 2, 4)
        basis = basis.reshape(KRY + 1, 1, 2, FIELDS, NBLK * BLK)
        return basis, table.reshape(2, KRY + 1, LANES)[:, :, :KRY]

    return jax.shard_map(
        local,
        mesh=mesh,
        in_specs=(
            P("mode", None, None, "space"),
            P(None, None, None, None, "space"),
            P(None, "space"),
            P("space"),
            P("space"),
            P("space"),
            P("space"),
            P("mode", "space"),
            P("space", None),
        ),
        out_specs=(P(None, "mode", None, None, "space"), P()),
        check_vma=False,
    )
```

time: 1310 us -> 141 us (0.11)
  blocking collectives: 963 us -> 0 us
  Pallas kernels: 0 us -> 136 us
  other arithmetic: 107 us -> 0 us
  local copies, waits for them, and re-layouts: 108 us -> 4.57 us
  starting transfers between devices: 51.1 us -> 0 us
  waiting for transfers between devices: 37.1 us -> 0 us
  matrix products: 33 us -> 0 us
    psum x10 -> x0, blocking collectives: 963 us -> none  [the longest x6 573 us: local(): lax.psum(local_inner(vectors[index], image), ('space', 'mode')) / count]
    pallas_call x0 -> x1, Pallas kernels: none -> 136 us  [local(): pl.pallas_call(functools.partial(kernel, space, modes), out_shape=(jax.Sh...]
    scatter-add x3 -> x0, other arithmetic: 63.2 us -> none  [local(): jax.ops.segment_sum(arrived, recv_target, num_segments=nblk + 1)[:nblk]]
    all_to_all x3 -> x0, starting transfers between devices: 33.4 us -> none  [local(): lax.all_to_all(buffer, 'space', split_axis=0, concat_axis=0, tiled=True)]
    dot_general x15 -> x0, matrix products: 33 us -> none  [the longest x3 15.4 us: local(): jnp.dot(flat, mortar, precision=HIGH, preferred_element_type=jnp.float32)]
    gather x18 -> x0, local copies, waits for them, and re-layouts: 29.6 us -> none  [the longest x6 15.5 us: local(): gathered = full[:, :, all_cols, :]]
    ppermute x6 -> x0, waiting for transfers between devices: 24.1 us -> none  [the longest x3 15.2 us: padded(): lax.ppermute(lax.slice_in_dim(block, block.shape[dim] - width, None, axis...]
    dot_general x6 -> x0, local copies, waits for them, and re-layouts: 21.4 us -> none  [local(): jnp.dot(flat, mortar, precision=HIGH, preferred_element_type=jnp.float32)]
  transfers between devices with their start and end apart: 9 -> 0, of which waited for: 5 -> 0; matrix products, arithmetic and copies ran while one was open for 4% -> 0% of each run, Pallas kernels for 0% -> 0%
where the time goes in v1:
time: 141 us
  Pallas kernels  136 us (96%)
  local copies, waits for them, and re-layouts  4.57 us (3%)
    pallas_call x1, Pallas kernels, local(): pl.pallas_call(functools.partial(kernel, space, modes), out_shape=(jax.Sh...  136 us

profile of v1, /device:TPU:1, one launch (start us, length us, event | category | flops | bytes accessed | tf_op | source)
XLA Modules:
  0.0 141.3 jit_solution(138833598695834403)
XLA Ops:
  0.6 1.1 reshape_squeeze.3
  1.7 0.0 copy-start
  1.7 0.2 copy.16
  1.9 0.0 copy-start.1
  1.9 0.0 copy-start.2
  1.9 0.0 copy-start.3
  1.9 0.0 copy-start.4
  1.9 0.0 copy-start.5
  2.0 0.0 copy-start.6
  2.0 0.0 copy-start.7
  2.0 0.2 reshape.31.field_ref
  2.2 0.5 copy-done
  2.7 0.0 copy-done.1
  2.7 0.0 copy-done.2
  2.7 0.0 copy-done.3
  2.7 0.0 copy-done.4
  2.7 0.0 copy-done.5
  2.7 0.0 copy-done.6
  2.7 0.0 copy-done.7
  2.7 136.0 %shard_map.104 = (f32[4,7,32,128]{3,2,1,0:T(8,128)S(1)}, f32[8,128]{1,0:T(8,128)S(1)}) custom-call(f32[7,32,128]{2,1,0:T(8,128)S(1)} %reshape.31.field_ref, f32[343,2,32]{2,1,0:T(2,128)S(1)} %bitcast.21, s32[6,32]{1,0:T(8,128)S(1)} %copy-done.2, s32[1,16]{1,0:T(1,128)S(1)} %bitcast.24, s32[1,128]{1,0:T(1,128)S(1)} %bitcast.25, s32[1,128]{1,0:T(1,128)S(1)} %bitcast.26, ...), custom_call_target="tpu_custom_call" | custom-call | tf_op jit(solution)/shard_map/pallas_call | solution.py:458
  138.7 0.7 copy.14
  139.4 0.5 reshape.37
  139.9 0.1 copy.12
  140.0 1.2 reshape.38
Async XLA Ops:
  1.7 1.0 copy-start
  1.9 0.8 copy-start.1
  1.9 0.8 copy-start.2
  1.9 0.8 copy-start.3
  1.9 0.8 copy-start.4
  1.9 0.8 copy-start.5
  2.0 0.8 copy-start.6
  2.0 0.8 copy-start.7

commit v2 on v1

--- a/solution.py
+++ b/solution.py
@@ -3,6 +3,7 @@
 
 import jax
 import jax.numpy as jnp
+import numpy as np
 from jax import lax
 from jax.experimental import pallas as pl
 from jax.experimental.pallas import tpu as pltpu
@@ -22,7 +23,7 @@
 OMEGA = 0.5
 EPS = 1e-06
 CHUNKS = 4
-STRIDE = 51
+LINE = 16
 ROW = 16
 
 
@@ -53,6 +54,42 @@
 
 def turn(x, sign):
     return pltpu.roll(x, BLK, axis=x.ndim - 1) * sign
+
+
+def two_sum(a, b):
+    total = a + b
+    part = total - a
+    return total, (a - (total - part)) + (b - part)
+
+
+def halves(x):
+    big = x * 4097.0
+    high = big - (big - x)
+    return high, x - high
+
+
+def two_product(a, b):
+    product = a[0] * b[0]
+    error = ((a[1] * b[1] - product) + a[1] * b[2] + a[2] * b[1]) + a[2] * b[2]
+    return product, error
+
+
+def ring(d, n):
+    return min(d, n - d)
+
+
+def sequence(space):
+    lines = space // LINE
+    rows = LINE // 2
+    every = [(z, y, c) for z in range(lines) for y in range(rows) for c in range(2)]
+    mixed = [every[i * 51 % space] for i in range(1, space)]
+    near = [o for o in mixed if o[0] == 0 or o[1:] == (0, 0)]
+    other = [o for o in mixed if o not in near]
+
+    def far(o):
+        return -ring(o[0], lines) - ring(o[1], rows)
+
+    return [(0, 0, 0)] + sorted(near, key=far) + sorted(other, key=far), len(near)
 
 
 def kernel(
@@ -67,6 +104,7 @@
     target_ref,
     phase_ref,
     mortar_ref,
+    order_ref,
     out_ref,
     hess_ref,
     sbuf,
@@ -82,6 +120,9 @@
     hmat,
     bdiag,
     image,
+    vector,
+    images,
+    ready,
     a2a_send,
     a2a_recv,
     halo_send,
@@ -91,37 +132,47 @@
 ):
     me = lax.axis_index("space")
     mode = lax.axis_index("mode")
-    line = 16
-    lines = space // line
+    lines = space // LINE
+    rows_y = LINE // 2
     wide_group = lines * modes
-    in_line = lax.rem(me, line)
-    my_line = me // line
+    in_line = lax.rem(me, LINE)
+    my_line = me // LINE
     in_wide = my_line * modes + mode
     chunk = space // CHUNKS
     count = float(space * modes * NBLK * BLK)
+    offsets, near = sequence(space)
+    z_part = [lax.rem(my_line + d, lines) * LINE for d in range(lines)]
+    y_part = [lax.rem(in_line // 2 + d, rows_y) * 2 for d in range(rows_y)]
+    c_part = [lax.rem(in_line + d, 2) for d in range(2)]
+    x_part = [lax.rem(mode + d, modes) for d in range(modes)]
 
     def partner(i):
-        return lax.rem(me + lax.rem(i * STRIDE, space), space)
-
-    def line_partner(o):
-        return {"space": my_line * line + lax.rem(in_line + o, line)}
-
-    def wide_partner(o):
-        there = lax.rem(in_wide + o, wide_group)
-        return {"space": there // modes * line + in_line, "mode": lax.rem(there, modes)}
+        z, y, c = offsets[i]
+        return {"space": z_part[z] + y_part[y] + c_part[c]}
+
+    line_partners = [
+        {"space": z_part[0] + y_part[y] + c_part[c]}
+        for y, c in sorted(
+            [(y, c) for y in range(rows_y) for c in range(2)][1:], key=lambda o: -ring(o[0], rows_y)
+        )
+    ]
+    wide_partners = [
+        {"space": z_part[z] + in_line, "mode": x_part[x]}
+        for z, x in sorted(
+            [(z, x) for z in range(lines) for x in range(modes)][1:],
+            key=lambda o: -ring(o[0], lines) - ring(o[1], modes),
+        )
+    ]
+
+    def shifted(code, way):
+        z = lax.rem(my_line + lines + way * (code // LINE), lines)
+        y = lax.rem(in_line // 2 + rows_y + way * lax.rem(code // 2, rows_y), rows_y)
+        c = lax.rem(in_line + lax.rem(code, 2), 2)
+        return z * LINE + y * 2 + c
 
     barrier = pltpu.get_barrier_semaphore()
-
-    def greet(i, c):
-        pl.semaphore_signal(barrier, inc=1, device_id={"space": partner(i)}, device_id_type=MESH)
-        return c
-
-    def greet_wide(o, c):
-        pl.semaphore_signal(barrier, inc=1, device_id=wide_partner(o), device_id_type=MESH)
-        return c
-
-    lax.fori_loop(1, space, greet, 0)
-    lax.fori_loop(1, wide_group, greet_wide, 0)
+    for there in wide_partners + line_partners:
+        pl.semaphore_signal(barrier, inc=1, device_id=there, device_id_type=MESH)
 
     lane = iota((1, LANES), 1)
     sign = jnp.where(lane < BLK, -1.0, 1.0).astype(F32)
@@ -133,7 +184,7 @@
     t_hi, t_lo = split(turned)
     for c in range(CHUNKS):
         row = iota((2 * chunk, 1), 0)
-        reader = partner(c * chunk + lax.rem(row, chunk))
+        reader = shifted(order_ref[2 * c * chunk : 2 * (c + 1) * chunk, :], 1)
         chosen = one_hot(slot_ref[...] == reader * 2 + row // chunk).astype(BF16)
         p_hi = matmul_nt(chosen, t_hi).astype(BF16)
         p_lo = matmul_nt(chosen, t_lo).astype(BF16)
@@ -147,7 +198,10 @@
     for t in range(KRY):
         rbuf[t, 0] = jnp.zeros((ROW, LANES), F32)
 
-    pl.semaphore_wait(barrier, space - 1 + wide_group - 1)
+    pl.semaphore_wait(barrier, LINE - 1 + wide_group - 1)
+    for z in range(1, lines):
+        there = {"space": z_part[z] + in_line}
+        pl.semaphore_signal(ready, inc=1, device_id=there, device_id_type=MESH)
 
     def send_halo(t, hi, lo):
         packed = matmul(hmat[...], jnp.concatenate([hi, lo], axis=0))
@@ -176,74 +230,122 @@
                     slot * chunk : (slot + 1) * chunk, k * LANES : (k + 1) * LANES
                 ]
 
-        def one(i, carry):
+        for i in range(max(1, c * chunk), (c + 1) * chunk):
+            if t == 0 and i == near + 1:
+                pl.semaphore_wait(ready, lines - 1)
             pltpu.make_async_remote_copy(
                 sbuf.at[t, i, pl.ds(0, 2 * FIELDS)],
                 rbuf.at[t, i, pl.ds(0, 2 * FIELDS)],
                 a2a_send.at[t, c],
                 a2a_recv.at[t, c],
-                device_id={"space": partner(i)},
+                device_id=partner(i),
                 device_id_type=MESH,
             ).start()
-            return carry
-
-        lax.fori_loop(1 if c == 0 else c * chunk, (c + 1) * chunk, one, 0)
 
     def wait_chunk(t, c, sem):
         number = chunk - 1 if c == 0 else chunk
         part = rbuf.at[t, pl.ds(0, number), pl.ds(0, 2 * FIELDS)]
         pltpu.make_async_copy(part, part, sem.at[t, c]).wait()
 
-    def start_sum(r, values):
-        vector = jnp.zeros((1, LANES), F32)
-        for n, value in enumerate(values):
-            vector = jnp.where(lane == n, value, vector)
-        first_buf[r, in_line] = vector
-
-        def one(o, carry):
+    def start_sum(r, row):
+        first_buf[r, in_line] = row
+        for there in line_partners:
             pltpu.make_async_remote_copy(
                 first_buf.at[r, in_line],
                 first_buf.at[r, in_line],
                 red_send.at[r, 0],
                 red_recv.at[r, 0],
-                device_id=line_partner(o),
+                device_id=there,
                 device_id_type=MESH,
             ).start()
-            return carry
-
-        lax.fori_loop(1, line, one, 0)
+
+    def add_rows(rows):
+        errors = jnp.zeros((1, LANES), F32)
+        while rows.shape[0] > 1:
+            half = rows.shape[0] // 2
+            rows, error = two_sum(rows[:half], rows[half:])
+            errors = errors + jnp.sum(error, axis=0)
+        return jnp.where(lane < BLK, rows[0], rows[0] + pltpu.roll(errors, BLK, axis=1))
 
     def middle_sum(r):
-        part = first_buf.at[r, pl.ds(0, line - 1)]
+        part = first_buf.at[r, pl.ds(0, LINE - 1)]
         pltpu.make_async_copy(part, part, red_recv.at[r, 0]).wait()
-        second_buf[r, in_wide] = jnp.sum(first_buf[r], axis=0)
-
-        def one(o, carry):
+        second_buf[r, in_wide] = add_rows(first_buf[r])
+        for there in wide_partners:
             pltpu.make_async_remote_copy(
                 second_buf.at[r, in_wide],
                 second_buf.at[r, in_wide],
                 red_send.at[r, 1],
                 red_recv.at[r, 1],
-                device_id=wide_partner(o),
+                device_id=there,
                 device_id_type=MESH,
             ).start()
-            return carry
-
-        lax.fori_loop(1, wide_group, one, 0)
 
     def end_sum(r, number):
         part = second_buf.at[r, pl.ds(0, wide_group - 1)]
         pltpu.make_async_copy(part, part, red_recv.at[r, 1]).wait()
-        total = jnp.sum(second_buf[r], axis=0) * (1.0 / count)
-        return [
-            jnp.sum(jnp.where(lane == n, total, 0.0), axis=1, keepdims=True) for n in range(number)
-        ]
-
-    def total(x):
-        return jnp.sum(jnp.sum(jnp.sum(x, axis=0), axis=0, keepdims=True), axis=1, keepdims=True)
-
-    def inner(left, right):
-        return [total(left * right), total(turn(left, sign) * right)]
+        row = add_rows(second_buf[r]) * (1.0 / count)
+
+        def pick(n):
+            return jnp.sum(jnp.where(lane == n, row, 0.0), axis=1, keepdims=True)
+
+        return [(pick(n), pick(BLK + n)) for n in range(number)]
+
+    def square_sum(x):
+        value = jnp.sum(jnp.sum(jnp.sum(x * x, axis=0), axis=0, keepdims=True), axis=1, keepdims=True)
+        return jnp.where(lane == 0, value, 0.0)
+
+    def products(left_refs, right_ref, square):
+        number = 2 * len(left_refs) + (1 if square else 0)
+        zero = jnp.zeros((8, LANES), F32)
+
+        def one(k, sums):
+            sums = list(sums)
+            for g in range(NBLK // 8):
+                part = slice(g * 8, (g + 1) * 8)
+
+                def parts(x):
+                    return (x,) + halves(x)
+
+                right = parts(right_ref[k, part, :])
+                pairs = []
+                for ref in left_refs:
+                    left = ref[k, part, :]
+                    pairs += [parts(left), parts(pltpu.roll(left, BLK, axis=1) * sign)]
+                if square:
+                    pairs.append(right)
+                for n, left in enumerate(pairs):
+                    value, error = two_product(left, right)
+                    sums[2 * n], lost = two_sum(sums[2 * n], value)
+                    sums[2 * n + 1] = sums[2 * n + 1] + (error + lost)
+            return tuple(sums)
+
+        sums = lax.fori_loop(0, FIELDS, one, (zero,) * (2 * number))
+        return [(sums[2 * n], sums[2 * n + 1]) for n in range(number)]
+
+    def fold(pair, axis, shift):
+        value, lost = two_sum(pair[0], pltpu.roll(pair[0], shift, axis=axis))
+        return value, pair[1] + pltpu.roll(pair[1], shift, axis=axis) + lost
+
+    def packed_sums(pairs):
+        sub = iota((8, LANES), 0)
+        across = iota((8, LANES), 1)
+        row = jnp.zeros((1, LANES), F32)
+        for start in range(0, len(pairs), 8):
+            merged = None
+            for n, pair in enumerate(pairs[start : start + 8]):
+                for shift in (4, 2, 1):
+                    pair = fold(pair, 0, shift)
+                if merged is None:
+                    merged = pair
+                else:
+                    merged = tuple(jnp.where(sub == n, a, b) for a, b in zip(pair, merged))
+            for shift in (64, 32, 16, 8, 4, 2, 1):
+                merged = fold(merged, 1, shift)
+            for n, part in enumerate(merged):
+                here = jnp.where(across == sub + (start + n * BLK), part, 0.0)
+                row = row + jnp.sum(here, axis=0, keepdims=True)
+        return row
 
     def minus(field, factor, vector):
         return field - factor[0] * vector - factor[1] * turn(vector, sign)
@@ -271,8 +373,7 @@
         block = one_hot(iota((NBLK, 2 * space), 0) == target_ref[...]).astype(BF16)
         for c in range(CHUNKS):
             row = iota((2 * chunk, 1), 0)
-            index = lax.rem((c * chunk + lax.rem(row, chunk)) * STRIDE, space)
-            writer = lax.rem(me + space - index, space)
+            writer = shifted(order_ref[2 * c * chunk : 2 * (c + 1) * chunk, :], -1)
             pick = one_hot(iota((2 * chunk, 2 * space), 1) == writer * 2 + row // chunk)
             there = matmul_nt(block, pick.astype(BF16)).astype(BF16)
             tmat[c] = jnp.concatenate([there, there], axis=1)
@@ -340,87 +441,104 @@
         m_hi, m_lo = split(bdiag[...])
         return matmul(hi, m_hi) + (matmul(lo, m_hi) + matmul(hi, m_lo))
 
-    def step(t, field, reduce_ops):
-        flatly = wide(field)
-        hi, lo = split(flatly)
-        send_halo(t, hi, lo)
-        reduce_ops[0]()
+    def swap(x):
+        other = pltpu.roll(x, BLK, axis=2)
+        sub = iota((FIELDS, NBLK, LANES), 1)
+        across = iota((FIELDS, NBLK, LANES), 2)
+        even = lax.rem(sub, 2) == 0
+        other = jnp.where(even, pltpu.roll(other, NBLK - 1, axis=1), pltpu.roll(other, 1, axis=1))
+        return jnp.where(even == (across < BLK), x, other)
+
+    def step(t, field, row_of_sums, then):
+        hi, lo = split(wide(field))
         i_hi, i_lo = split(wide(turn(field, sign)))
         rows = jnp.concatenate([hi, i_hi, hi, i_hi, lo, i_lo], axis=0)
-        for c in range(CHUNKS):
-            send_chunk(t, c, rows)
-            if c + 1 < len(reduce_ops):
-                reduce_ops[c + 1]()
+        send_chunk(t, 0, rows)
+        start_sum(t, row_of_sums())
+        send_halo(t, hi, lo)
+        send_chunk(t, 1, rows)
+        send_chunk(t, 2, rows)
+        middle_sum(t)
+        send_chunk(t, 3, rows)
         if t == 0:
             prepare()
         totals = flux(t, field, hi, lo)
+        then()
         mortared = arrived(t)
         return jnp.stack(
             [totals[k] + mortared[k * NBLK : (k + 1) * NBLK] for k in range(FIELDS)]
         )
 
     hess = []
-    forcing = field_ref[...]
+    gram = {}
     state = {}
 
-    def end_first():
-        state["first"] = jnp.sqrt(end_sum(0, 1)[0] + EPS)
-
-    image0 = step(
-        0,
-        forcing,
-        [
-            lambda: start_sum(0, [total(forcing * forcing)]),
-            lambda: middle_sum(0),
-            lambda: None,
-            end_first,
-        ],
-    )
+    def gram_products(t):
+        own = products([], vector.at[t], True)
+        return own + (products([vector.at[i] for i in range(t)], vector.at[t], False) if t else [])
+
+    def image_products(t):
+        return products([vector.at[i] for i in range(t + 1)], images.at[t], True)
+
+    def new_vector(t):
+        number = 2 * (t + 1)
+        sums = [two_sum(*pair) for pair in end_sum(t + 1, number + 2 + 2 * t)]
+        gram[t, t] = (sums[number + 1][0] - 1.0) + sums[number + 1][1]
+        for i in range(t):
+            gram[i, t] = (sums[number + 2 + 2 * i][0], sums[number + 3 + 2 * i][0])
+        value, lost = sums[number]
+        factors = []
+        for i in range(t + 1):
+            for part in range(2):
+                h, rest = sums[2 * i + part]
+                whole = (h,) + halves(h)
+                square, error = two_product(whole, whole)
+                value, missed = two_sum(value, -square)
+                lost = lost + (missed - error - 2.0 * h * rest + square * gram[i, i])
+            factors.append((sums[2 * i][0], sums[2 * i + 1][0]))
+        for k in range(t + 1):
+            for i in range(k):
+                (a, b), (c, d), (g, f) = factors[i], factors[k], gram[i, k]
+                lost = lost + 2.0 * ((a * c + b * d) * g - (a * d - b * c) * f)
+        length = jnp.sqrt(jnp.maximum(value + lost, 0.0) + EPS)
+        rest = images[t]
+        for i in range(t + 1):
+            rest = minus(rest, factors[i], vector[i])
+        hess.append((factors, length))
+        return rest / length
+
+    forcing = swap(field_ref[...])
+
+    def first_vector():
+        first = jnp.sqrt(end_sum(0, 1)[0][0] + EPS)
+        state["first"] = first
+        vector[0] = forcing / first
+        out_ref[0] = swap(vector[0])
+        state["gram"] = gram_products(0)
+
+    plain = step(0, forcing, lambda: square_sum(forcing), first_vector)
     first = state["first"]
-    out_ref[0] = forcing / first
-    images = [jnp.where(first < jnp.inf, image0 / first, 0.0)]
-    vectors = 1
-
-    for t in range(1, KRY + 1):
-        w = images[t - 1]
-
-        def start_products(t=t, w=w):
-            products = []
-            for index in range(t):
-                products += inner(out_ref[index], w)
-            start_sum(2 * t - 1, products)
-
-        def end_products(t=t, w=w):
-            values = end_sum(2 * t - 1, 2 * t)
-            factors = [(values[2 * n], values[2 * n + 1]) for n in range(t)]
-            rest = w
-            for index in range(t):
-                rest = minus(rest, factors[index], out_ref[index])
-            out_ref[t] = rest
-            state["factors"] = factors
-            start_sum(2 * t, [total(rest * rest)])
-
-        def end_norm(t=t):
-            length = jnp.sqrt(end_sum(2 * t, 1)[0] + EPS)
-            state["length"] = length
-            out_ref[t] = out_ref[t] / length
-
-        middle = [
-            lambda t=t: middle_sum(2 * t - 1),
-            end_products,
-            lambda t=t: middle_sum(2 * t),
-        ]
-        if t < KRY:
-            plain = step(t, w, [start_products] + middle + [end_norm])
-        else:
-            for op in [start_products] + middle + [end_norm]:
-                op()
-        factors, length = state["factors"], state["length"]
-        hess.append((factors, length))
-        if t < KRY:
-            for index in range(t):
-                plain = minus(plain, factors[index], images[index])
-            images.append(plain / length)
+    images[0] = jnp.where(first < jnp.inf, plain / first, 0.0)
+
+    for t in range(1, KRY):
+
+        def sums(t=t):
+            return packed_sums(image_products(t - 1) + state["gram"])
+
+        def next_vector(t=t):
+            vector[t] = new_vector(t - 1)
+            out_ref[t] = swap(vector[t])
+            state["gram"] = gram_products(t)
+
+        plain = step(t, images[t - 1], sums, next_vector)
+        factors, length = hess[t - 1]
+        for i in range(t):
+            plain = minus(plain, factors[i], images[i])
+        images[t] = plain / length
+
+    start_sum(KRY, packed_sums(image_products(KRY - 1) + state["gram"]))
+    middle_sum(KRY)
+    out_ref[KRY] = swap(new_vector(KRY - 1))
 
     row = iota((8, LANES), 0)
     column = iota((8, LANES), 1)
@@ -437,8 +555,8 @@
             halo_copy(t, side, halo_send).wait()
         for c in range(CHUNKS):
             wait_chunk(t, c, a2a_send)
-    for r in range(2 * KRY + 1):
-        part = first_buf.at[r, pl.ds(0, line - 1)]
+    for r in range(KRY + 1):
+        part = first_buf.at[r, pl.ds(0, LINE - 1)]
         pltpu.make_async_copy(part, part, red_send.at[r, 0]).wait()
         part = second_buf.at[r, pl.ds(0, wide_group - 1)]
         pltpu.make_async_copy(part, part, red_send.at[r, 1]).wait()
@@ -446,12 +564,15 @@
 
 def solution(mesh):
     space, modes = mesh.shape["space"], mesh.shape["mode"]
-    wide_group = space // 16 * modes
-    sums = 2 * KRY + 1
+    wide_group = space // LINE * modes
+    sums = KRY + 1
+    chunk = space // CHUNKS
+    codes = np.array([(z * LINE + y * 2 + c) for z, y, c in sequence(space)[0]], np.int32)
+    codes = np.repeat(codes.reshape(CHUNKS, 1, chunk), 2, axis=1).reshape(2 * space, 1)
     dma = pltpu.SemaphoreType.DMA
 
     def local(right, jac, cols, halo, blocks, slot, target, phase, mortar):
-        field = right[0].reshape(2, FIELDS, NBLK, BLK).transpose(1, 2, 0, 3)
+        field = right[0].reshape(2, FIELDS, NBLK // 2, LANES).transpose(1, 2, 0, 3)
         field = field.reshape(FIELDS, NBLK, LANES)
         jac = jac.transpose(1, 2, 3, 0, 4).reshape(FIELDS**3, 2, NBLK)
         vmem = pl.BlockSpec(memory_space=pltpu.VMEM)
@@ -461,14 +582,14 @@
                 jax.ShapeDtypeStruct((KRY + 1, FIELDS, NBLK, LANES), F32),
                 jax.ShapeDtypeStruct((8, LANES), F32),
             ),
-            in_specs=[vmem] * 9,
+            in_specs=[vmem] * 10,
             out_specs=(vmem, vmem),
             scratch_shapes=[
                 pltpu.VMEM((KRY, space, ROW, LANES), F32),
                 pltpu.VMEM((KRY, space, ROW, LANES), F32),
                 pltpu.VMEM((KRY, FIELDS, HB, LANES), F32),
                 pltpu.VMEM((KRY, 2, FIELDS, HB, LANES), F32),
-                pltpu.VMEM((sums, 16, 1, LANES), F32),
+                pltpu.VMEM((sums, LINE, 1, LANES), F32),
                 pltpu.VMEM((sums, wide_group, 1, LANES), F32),
                 pltpu.VMEM((FIELDS**3, 2, NBLK, LANES), F32),
                 pltpu.VMEM((CHUNKS, 2 * space // CHUNKS, 6 * NBLK), BF16),
@@ -477,6 +598,9 @@
                 pltpu.VMEM((HB, 2 * NBLK), BF16),
                 pltpu.VMEM((LANES, LANES), F32),
                 pltpu.VMEM((FIELDS, FIELDS, NBLK, LANES), F32),
+                pltpu.VMEM((KRY, FIELDS, NBLK, LANES), F32),
+                pltpu.VMEM((KRY, FIELDS, NBLK, LANES), F32),
+                pltpu.SemaphoreType.REGULAR,
                 dma((KRY, CHUNKS)),
                 dma((KRY, CHUNKS)),
                 dma((KRY, 2)),
@@ -497,8 +621,9 @@
             target.reshape(1, 2 * space),
             phase,
             mortar,
+            jnp.asarray(codes),
         )
-        basis = basis.reshape(KRY + 1, FIELDS, NBLK, 2, BLK).transpose(0, 3, 1, 2, 4)
+        basis = basis.reshape(KRY + 1, FIELDS, NBLK // 2, 2, LANES).transpose(0, 3, 1, 2, 4)
         basis = basis.reshape(KRY + 1, 1, 2, FIELDS, NBLK * BLK)
         return basis, table.reshape(2, KRY + 1, LANES)[:, :, :KRY]
 

time: 141 us -> 120 us (0.85)
  Pallas kernels: 136 us -> 113 us
    pallas_call x1, Pallas kernels: 136 us -> 113 us  [local(): pl.pallas_call(functools.partial(kernel, space, modes), out_shape=(jax.Sh...]
    unnamed x17 -> x22, local copies, waits for them, and re-layouts: 1.26 us -> 5.67 us
    reshape x3 -> x0, local copies, waits for them, and re-layouts: 1.94 us -> none  [the longest x1 1.24 us: local(): basis = basis.reshape(KRY + 1, 1, 2, FIELDS, NBLK * BLK)]
where the time goes in v2:
time: 120 us
  Pallas kernels  113 us (94%)
  local copies, waits for them, and re-layouts  5.67 us (5%)
    pallas_call x1, Pallas kernels, local(): pl.pallas_call(functools.partial(kernel, space, modes), out_shape=(jax.Sh...  113 us
    unnamed x22, local copies, waits for them, and re-layouts  5.67 us

profile of v2, /device:TPU:1, one launch (start us, length us, event | category | flops | bytes accessed | tf_op | source)
XLA Modules:
  0.0 119.9 jit_solution(11914673217578063214)
XLA Ops:
  0.6 0.0 copy-start.4
  0.6 0.0 copy-start.7
  0.7 0.0 copy-start.8
  0.7 0.0 copy-start.9
  0.7 0.0 copy-start.5
  0.7 0.0 copy-start.6
  0.7 0.6 copy-done.4
  1.3 0.0 copy-done.7
  1.3 0.0 copy-done.8
  1.3 0.0 copy-done.9
  1.3 0.0 copy-done.5
  1.4 0.0 copy-done.6
  1.4 0.0 copy-start
  1.4 1.0 copy-done
  2.4 0.0 copy-start.1
  2.4 0.9 copy-done.1
  3.3 0.0 copy-start.2
  3.3 0.9 copy-done.2
  4.2 0.0 copy-start.3
  4.2 0.8 copy-done.3
  4.9 113.5 %shard_map.113 = (f32[4,7,32,128]{3,2,1,0:T(8,128)S(1)}, f32[8,128]{1,0:T(8,128)S(1)}) custom-call(f32[7,32,128]{2,1,0:T(8,128)S(1)} %bitcast.21, f32[343,2,32]{2,1,0:T(2,128)S(1)} %bitcast.20, s32[6,32]{1,0:T(8,128)S(1)} %copy-done.4, s32[1,16]{1,0:T(1,128)S(1)} %bitcast.24, s32[1,128]{1,0:T(1,128)S(1)} %bitcast.25, s32[1,128]{1,0:T(1,128)S(1)} %bitcast.26, ...), custom_call_target="tpu_custom_call" | custom-call | tf_op jit(solution)/shard_map/pallas_call | solution.py:579
  118.4 0.7 copy.15
  119.1 0.8 copy.17
Async XLA Ops:
  0.6 0.7 copy-start.4
  0.6 0.7 copy-start.7
  0.7 0.7 copy-start.8
  0.7 0.7 copy-start.9
  0.7 0.7 copy-start.5
  0.7 0.7 copy-start.6
  1.4 1.0 copy-start
  2.4 0.9 copy-start.1
  3.3 0.9 copy-start.2
  4.2 0.8 copy-start.3

commit v3 on v2

--- a/solution.py
+++ b/solution.py
@@ -83,18 +83,24 @@
     rows = LINE // 2
     every = [(z, y, c) for z in range(lines) for y in range(rows) for c in range(2)]
     mixed = [every[i * 51 % space] for i in range(1, space)]
-    near = [o for o in mixed if o[0] == 0 or o[1:] == (0, 0)]
-    other = [o for o in mixed if o not in near]
-
-    def far(o):
-        return -ring(o[0], lines) - ring(o[1], rows)
-
-    return [(0, 0, 0)] + sorted(near, key=far) + sorted(other, key=far), len(near)
+    return [(0, 0, 0)] + sorted(mixed, key=lambda o: -ring(o[0], lines) - ring(o[1], rows))
 
 
 def kernel(
     space,
     modes,
+    field_hbm,
+    jac_hbm,
+    cols_hbm,
+    halo_hbm,
+    blocks_hbm,
+    slot_hbm,
+    target_hbm,
+    phase_hbm,
+    mortar_hbm,
+    order_hbm,
+    out_ref,
+    hess_ref,
     field_ref,
     jac_ref,
     cols_ref,
@@ -105,8 +111,7 @@
     phase_ref,
     mortar_ref,
     order_ref,
-    out_ref,
-    hess_ref,
+    in_sem,
     sbuf,
     rbuf,
     hsend,
@@ -120,6 +125,7 @@
     hmat,
     bdiag,
     image,
+    own_part,
     vector,
     images,
     ready,
@@ -140,7 +146,7 @@
     in_wide = my_line * modes + mode
     chunk = space // CHUNKS
     count = float(space * modes * NBLK * BLK)
-    offsets, near = sequence(space)
+    offsets = sequence(space)
     z_part = [lax.rem(my_line + d, lines) * LINE for d in range(lines)]
     y_part = [lax.rem(in_line // 2 + d, rows_y) * 2 for d in range(rows_y)]
     c_part = [lax.rem(in_line + d, 2) for d in range(2)]
@@ -170,6 +176,26 @@
         c = lax.rem(in_line + lax.rem(code, 2), 2)
         return z * LINE + y * 2 + c
 
+    copies = [
+        pltpu.make_async_copy(source, there, in_sem.at[n])
+        for n, (source, there) in enumerate(
+            [
+                (slot_hbm, slot_ref),
+                (blocks_hbm, blocks_ref),
+                (phase_hbm, phase_ref),
+                (order_hbm, order_ref),
+                (halo_hbm, halo_ref),
+                (field_hbm, field_ref),
+                (cols_hbm, cols_ref),
+                (target_hbm, target_ref),
+                (mortar_hbm, mortar_ref),
+                (jac_hbm, jac_ref),
+            ]
+        )
+    ]
+    for copy in copies:
+        copy.start()
+
     barrier = pltpu.get_barrier_semaphore()
     for there in wide_partners + line_partners:
         pl.semaphore_signal(barrier, inc=1, device_id=there, device_id_type=MESH)
@@ -178,6 +204,8 @@
     sign = jnp.where(lane < BLK, -1.0, 1.0).astype(F32)
     level = (mode + 1).astype(F32)
 
+    for copy in copies[:5]:
+        copy.wait()
     angle = phase_ref[...].astype(F32) * (level * (2.0 * math.pi / NPHASE))
     picked = one_hot(iota((NBLK, LANES), 0) == blocks_ref[...])
     turned = jnp.concatenate([picked * jnp.cos(angle), picked * jnp.sin(angle)], axis=0)
@@ -198,10 +226,11 @@
     for t in range(KRY):
         rbuf[t, 0] = jnp.zeros((ROW, LANES), F32)
 
-    pl.semaphore_wait(barrier, LINE - 1 + wide_group - 1)
-    for z in range(1, lines):
-        there = {"space": z_part[z] + in_line}
-        pl.semaphore_signal(ready, inc=1, device_id=there, device_id_type=MESH)
+    def enter():
+        pl.semaphore_wait(barrier, LINE - 1 + wide_group - 1)
+        for z in range(1, lines):
+            there = {"space": z_part[z] + in_line}
+            pl.semaphore_signal(ready, inc=1, device_id=there, device_id_type=MESH)
 
     def send_halo(t, hi, lo):
         packed = matmul(hmat[...], jnp.concatenate([hi, lo], axis=0))
@@ -221,7 +250,7 @@
     def halo_copy(t, side, sem):
         return pltpu.make_async_copy(hsend.at[t], hrecv.at[t, side], sem.at[t, side])
 
-    def send_chunk(t, c, rows):
+    def pack(t, c, rows):
         packed = matmul(pmat[c], rows)
         flat = sbuf.at[t].reshape(space * ROW, LANES)
         for slot in range(2):
@@ -230,14 +259,13 @@
                     slot * chunk : (slot + 1) * chunk, k * LANES : (k + 1) * LANES
                 ]
 
-        for i in range(max(1, c * chunk), (c + 1) * chunk):
-            if t == 0 and i == near + 1:
-                pl.semaphore_wait(ready, lines - 1)
+    def send(t, places):
+        for i in places:
             pltpu.make_async_remote_copy(
                 sbuf.at[t, i, pl.ds(0, 2 * FIELDS)],
                 rbuf.at[t, i, pl.ds(0, 2 * FIELDS)],
-                a2a_send.at[t, c],
-                a2a_recv.at[t, c],
+                a2a_send.at[t, i // chunk],
+                a2a_recv.at[t, i // chunk],
                 device_id=partner(i),
                 device_id_type=MESH,
             ).start()
@@ -351,6 +379,8 @@
         return field - factor[0] * vector - factor[1] * turn(vector, sign)
 
     def prepare():
+        for copy in copies[6:]:
+            copy.wait()
         ones = jnp.ones((1, LANES), F32)
         for h in range(2):
             part = jac_ref[:, h, :]
@@ -365,7 +395,9 @@
                         value = columns[:, q : q + 1]
                         if j == 0 and o == i:
                             value = value + (SHIFT if h == 0 else OMEGA * level)
-                        coef[q, h] = value * (ones if h == 0 else sign)
+                        value = value * (ones if h == 0 else sign)
+                        for g in range(NBLK // 8):
+                            coef[j, g, (i * FIELDS + o) * 2 + h] = value[g * 8 : (g + 1) * 8]
         for j in range(FIELDS - 1):
             source = one_hot(iota((2 * NBLK, NBLK), 0) == cols_ref[j : j + 1, :]).astype(BF16)
             there = matmul_nt(eye, source).astype(BF16)
@@ -393,53 +425,55 @@
         )
         gathered = matmul(nmat[...], sources)
         for k in range(FIELDS):
-            image[0, k] = field[k]
-            for j in range(FIELDS - 1):
-                image[j + 1, k] = gathered[j * NBLK : (j + 1) * NBLK, k * LANES : (k + 1) * LANES]
-
-        def one(n, totals):
-            j = n // FIELDS
-            i = lax.rem(n, FIELDS)
-            value = image[j, i]
-            other = pltpu.roll(value, BLK, axis=1)
-            return tuple(
-                totals[o]
-                + coef[o * FIELDS * FIELDS + i * FIELDS + j, 0] * value
-                + coef[o * FIELDS * FIELDS + i * FIELDS + j, 1] * other
-                for o in range(FIELDS)
-            )
-
-        zero = jnp.zeros((NBLK, LANES), F32)
-        return lax.fori_loop(0, FIELDS * FIELDS, one, (zero,) * FIELDS)
-
-    def arrived(t):
-        sums = jnp.zeros((NBLK, FIELDS * LANES), F32)
+            tile = jnp.concatenate([field[k], gathered[:, k * LANES : (k + 1) * LANES]], axis=0)
+            image[0, k] = tile
+            image[1, k] = pltpu.roll(tile, BLK, axis=1)
+
+        for g in range(NBLK // 8):
+
+            def one(j, sums, g=g):
+                sums = list(sums)
+                here = pl.ds(pl.multiple_of(j * NBLK + g * 8, 8), 8)
+                factor = coef.at[j, g]
+                for i in range(FIELDS):
+                    value = image[0, i, here, :]
+                    other = image[1, i, here, :]
+                    for o in range(FIELDS):
+                        n = 2 * (i * FIELDS + o)
+                        sums[o] = sums[o] + (factor[n] * value + factor[n + 1] * other)
+                return tuple(sums)
+
+            sums = lax.fori_loop(0, FIELDS, one, (jnp.zeros((8, LANES), F32),) * FIELDS)
+            for o in range(FIELDS):
+                own_part[o, g * 8 : (g + 1) * 8, :] = sums[o]
+
+    def arrived(t, c):
+        wait_chunk(t, c, a2a_recv)
         flat = rbuf.at[t].reshape(space * ROW, LANES)
-        for c in range(CHUNKS):
-            wait_chunk(t, c, a2a_recv)
-            rows = jnp.concatenate(
-                [
-                    jnp.concatenate(
-                        [
-                            flat[
-                                pl.ds(c * chunk * ROW + slot * FIELDS + k, chunk, stride=ROW), :
-                            ]
-                            for k in range(FIELDS)
-                        ],
-                        axis=1,
-                    )
-                    for slot in range(2)
-                ],
-                axis=0,
-            )
-            hi, lo = split(rows)
-            sums = sums + matmul(tmat[c], jnp.concatenate([hi, lo], axis=0))
+        rows = jnp.concatenate(
+            [
+                jnp.concatenate(
+                    [
+                        flat[pl.ds(c * chunk * ROW + slot * FIELDS + k, chunk, stride=ROW), :]
+                        for k in range(FIELDS)
+                    ],
+                    axis=1,
+                )
+                for slot in range(2)
+            ],
+            axis=0,
+        )
+        hi, lo = split(rows)
+        return matmul(tmat[c], jnp.concatenate([hi, lo], axis=0))
+
+    def mortared(sums):
         rows = jnp.concatenate(
             [sums[:, k * LANES : (k + 1) * LANES] for k in range(FIELDS)], axis=0
         )
         hi, lo = split(rows)
         m_hi, m_lo = split(bdiag[...])
-        return matmul(hi, m_hi) + (matmul(lo, m_hi) + matmul(hi, m_lo))
+        out = matmul(hi, m_hi) + (matmul(lo, m_hi) + matmul(hi, m_lo))
+        return out.reshape(FIELDS, NBLK, LANES)
 
     def swap(x):
         other = pltpu.roll(x, BLK, axis=2)
@@ -453,21 +487,38 @@
         hi, lo = split(wide(field))
         i_hi, i_lo = split(wide(turn(field, sign)))
         rows = jnp.concatenate([hi, i_hi, hi, i_hi, lo, i_lo], axis=0)
-        send_chunk(t, 0, rows)
-        start_sum(t, row_of_sums())
-        send_halo(t, hi, lo)
-        send_chunk(t, 1, rows)
-        send_chunk(t, 2, rows)
-        middle_sum(t)
-        send_chunk(t, 3, rows)
         if t == 0:
+            for c in range(CHUNKS):
+                pack(t, c, rows)
+            row = row_of_sums()
+            enter()
+            start_sum(t, row)
+            near = [i for i in range(1, space) if offsets[i][0] == 0 or offsets[i][1:] == (0, 0)]
+            other = [i for i in range(1, space) if i not in near]
+            send(t, near)
+            pl.semaphore_wait(ready, lines - 1)
+            send_halo(t, hi, lo)
+            send(t, other[: space // 4])
+            middle_sum(t)
+            send(t, other[space // 4 :])
             prepare()
-        totals = flux(t, field, hi, lo)
+        else:
+            pack(t, 0, rows)
+            send(t, range(1, chunk))
+            start_sum(t, row_of_sums())
+            pack(t, 1, rows)
+            send(t, range(chunk, 2 * chunk))
+            send_halo(t, hi, lo)
+            middle_sum(t)
+            for c in range(2, CHUNKS):
+                pack(t, c, rows)
+                send(t, range(c * chunk, (c + 1) * chunk))
+        flux(t, field, hi, lo)
+        sums = arrived(t, 0) + arrived(t, 1)
         then()
-        mortared = arrived(t)
-        return jnp.stack(
-            [totals[k] + mortared[k * NBLK : (k + 1) * NBLK] for k in range(FIELDS)]
-        )
+        sums = sums + arrived(t, 2)
+        sums = sums + arrived(t, 3)
+        return own_part[...] + mortared(sums)
 
     hess = []
     gram = {}
@@ -507,13 +558,14 @@
         hess.append((factors, length))
         return rest / length
 
+    for copy in copies[5:6]:
+        copy.wait()
     forcing = swap(field_ref[...])
 
     def first_vector():
         first = jnp.sqrt(end_sum(0, 1)[0][0] + EPS)
         state["first"] = first
         vector[0] = forcing / first
-        out_ref[0] = swap(vector[0])
         state["gram"] = gram_products(0)
 
     plain = step(0, forcing, lambda: square_sum(forcing), first_vector)
@@ -527,7 +579,6 @@
 
         def next_vector(t=t):
             vector[t] = new_vector(t - 1)
-            out_ref[t] = swap(vector[t])
             state["gram"] = gram_products(t)
 
         plain = step(t, images[t - 1], sums, next_vector)
@@ -537,6 +588,8 @@
         images[t] = plain / length
 
     start_sum(KRY, packed_sums(image_products(KRY - 1) + state["gram"]))
+    for t in range(KRY):
+        out_ref[t] = swap(vector[t])
     middle_sum(KRY)
     out_ref[KRY] = swap(new_vector(KRY - 1))
 
@@ -567,7 +620,7 @@
     wide_group = space // LINE * modes
     sums = KRY + 1
     chunk = space // CHUNKS
-    codes = np.array([(z * LINE + y * 2 + c) for z, y, c in sequence(space)[0]], np.int32)
+    codes = np.array([(z * LINE + y * 2 + c) for z, y, c in sequence(space)], np.int32)
     codes = np.repeat(codes.reshape(CHUNKS, 1, chunk), 2, axis=1).reshape(2 * space, 1)
     dma = pltpu.SemaphoreType.DMA
 
@@ -582,22 +635,34 @@
                 jax.ShapeDtypeStruct((KRY + 1, FIELDS, NBLK, LANES), F32),
                 jax.ShapeDtypeStruct((8, LANES), F32),
             ),
-            in_specs=[vmem] * 10,
+            in_specs=[pl.BlockSpec(memory_space=pltpu.HBM)] * 10,
             out_specs=(vmem, vmem),
             scratch_shapes=[
+                pltpu.VMEM((FIELDS, NBLK, LANES), F32),
+                pltpu.VMEM((FIELDS**3, 2, NBLK), F32),
+                pltpu.VMEM((FIELDS - 1, NBLK), jnp.int32),
+                pltpu.VMEM((1, HB), jnp.int32),
+                pltpu.VMEM((1, LANES), jnp.int32),
+                pltpu.VMEM((1, LANES), jnp.int32),
+                pltpu.VMEM((1, 2 * space), jnp.int32),
+                pltpu.VMEM((1, LANES), jnp.int32),
+                pltpu.VMEM((BLK, BLK), F32),
+                pltpu.VMEM((2 * space, 1), jnp.int32),
+                dma((10,)),
                 pltpu.VMEM((KRY, space, ROW, LANES), F32),
                 pltpu.VMEM((KRY, space, ROW, LANES), F32),
                 pltpu.VMEM((KRY, FIELDS, HB, LANES), F32),
                 pltpu.VMEM((KRY, 2, FIELDS, HB, LANES), F32),
                 pltpu.VMEM((sums, LINE, 1, LANES), F32),
                 pltpu.VMEM((sums, wide_group, 1, LANES), F32),
-                pltpu.VMEM((FIELDS**3, 2, NBLK, LANES), F32),
+                pltpu.VMEM((FIELDS, NBLK // 8, 2 * FIELDS * FIELDS, 8, LANES), F32),
                 pltpu.VMEM((CHUNKS, 2 * space // CHUNKS, 6 * NBLK), BF16),
                 pltpu.VMEM((CHUNKS, NBLK, 4 * space // CHUNKS), BF16),
                 pltpu.VMEM(((FIELDS - 1) * NBLK, 4 * NBLK), BF16),
                 pltpu.VMEM((HB, 2 * NBLK), BF16),
                 pltpu.VMEM((LANES, LANES), F32),
-                pltpu.VMEM((FIELDS, FIELDS, NBLK, LANES), F32),
+                pltpu.VMEM((2, FIELDS, FIELDS * NBLK, LANES), F32),
+                pltpu.VMEM((FIELDS, NBLK, LANES), F32),
                 pltpu.VMEM((KRY, FIELDS, NBLK, LANES), F32),
                 pltpu.VMEM((KRY, FIELDS, NBLK, LANES), F32),
                 pltpu.SemaphoreType.REGULAR,
@@ -609,7 +674,7 @@
                 dma((sums, 2)),
             ],
             compiler_params=pltpu.CompilerParams(
-                collective_id=0, has_side_effects=True, vmem_limit_bytes=48 << 20
+                collective_id=0, has_side_effects=True, vmem_limit_bytes=64 << 20
             ),
         )(
             field,

time: 120 us -> 112 us (0.933)
  Pallas kernels: 113 us -> 108 us
  local copies, waits for them, and re-layouts: 5.67 us -> 3.16 us
    pallas_call x1, Pallas kernels: 113 us -> 108 us  [local(): pl.pallas_call(functools.partial(kernel, space, modes), out_shape=(jax.Sh...]
    unnamed x22 -> x4, local copies, waits for them, and re-layouts: 5.67 us -> 3.16 us
where the time goes in v3:
time: 112 us
  Pallas kernels  108 us (96%)
  local copies, waits for them, and re-layouts  3.16 us (3%)
    pallas_call x1, Pallas kernels, local(): pl.pallas_call(functools.partial(kernel, space, modes), out_shape=(jax.Sh...  108 us
    unnamed x4, local copies, waits for them, and re-layouts  3.16 us

profile of v3, /device:TPU:1, one launch (start us, length us, event | category | flops | bytes accessed | tf_op | source)
XLA Modules:
  0.0 111.6 jit_solution(4930002222450961809)
XLA Ops:
  0.6 107.8 %shard_map.113 = (f32[4,7,32,128]{3,2,1,0:T(8,128)}, f32[8,128]{1,0:T(8,128)}) custom-call(f32[7,32,128]{2,1,0:T(8,128)} %bitcast.21, f32[343,2,32]{2,1,0:T(2,128)} %bitcast.20, s32[6,32]{1,0:T(8,128)} %cols_hbm.1, s32[1,16]{1,0:T(1,128)} %bitcast.24, s32[1,128]{1,0:T(1,128)} %bitcast.25, s32[1,128]{1,0:T(1,128)} %bitcast.26, s32[1,256]{1,0:T(1,128)} %bitcast.23, ...), custom_call_target="tpu_custom_call" | custom-call | tf_op jit(solution)/shard_map/pallas_call | solution.py:632
  108.4 0.0 copy-start
  108.4 0.7 copy-done
  109.1 0.7 copy.15
  109.8 1.8 %copy.17 = f32[4,1,2,7,2048]{4,2,3,1,0:T(2,128)} copy(f32[4,1,2,7,2048]{4,2,3,1,0:T(2,128)} %bitcast.19) | data formatting | bytes 917504
Async XLA Ops:
  108.4 0.7 copy-start

commit v4 on v3

--- a/solution.py
+++ b/solution.py
@@ -193,12 +193,11 @@
             ]
         )
     ]
-    for copy in copies:
-        copy.start()
-
     barrier = pltpu.get_barrier_semaphore()
     for there in wide_partners + line_partners:
         pl.semaphore_signal(barrier, inc=1, device_id=there, device_id_type=MESH)
+    for copy in copies:
+        copy.start()
 
     lane = iota((1, LANES), 1)
     sign = jnp.where(lane < BLK, -1.0, 1.0).astype(F32)
@@ -593,15 +592,14 @@
     middle_sum(KRY)
     out_ref[KRY] = swap(new_vector(KRY - 1))
 
-    row = iota((8, LANES), 0)
-    column = iota((8, LANES), 1)
-    table = jnp.zeros((8, LANES), F32)
+    row = iota((2, KRY + 1), 0)
+    column = iota((2, KRY + 1), 1)
     for j, (factors, length) in enumerate(hess):
+        table = jnp.zeros((2, KRY + 1), F32)
         for index, factor in enumerate(factors):
             for part in range(2):
-                table = jnp.where((row == part * 4 + index) & (column == j), factor[part], table)
-        table = jnp.where((row == j + 1) & (column == j), length, table)
-    hess_ref[...] = table
+                table = jnp.where((row == part) & (column == index), factor[part], table)
+        hess_ref[j] = jnp.where((row == 0) & (column == j + 1), length, table)
 
     for t in range(KRY):
         for side in range(2):
@@ -633,7 +631,7 @@
             functools.partial(kernel, space, modes),
             out_shape=(
                 jax.ShapeDtypeStruct((KRY + 1, FIELDS, NBLK, LANES), F32),
-                jax.ShapeDtypeStruct((8, LANES), F32),
+                jax.ShapeDtypeStruct((KRY, 2, KRY + 1), F32),
             ),
             in_specs=[pl.BlockSpec(memory_space=pltpu.HBM)] * 10,
             out_specs=(vmem, vmem),
@@ -690,7 +688,7 @@
         )
         basis = basis.reshape(KRY + 1, FIELDS, NBLK // 2, 2, LANES).transpose(0, 3, 1, 2, 4)
         basis = basis.reshape(KRY + 1, 1, 2, FIELDS, NBLK * BLK)
-        return basis, table.reshape(2, KRY + 1, LANES)[:, :, :KRY]
+        return basis, table.transpose(1, 2, 0)
 
     return jax.shard_map(
         local,

time: 112 us -> 112 us (level)
  no operation moved by 1% of the time
where the time goes in v4:
time: 112 us; the launch traced here: 111 us
  Pallas kernels  108 us (96%)
  local copies, waits for them, and re-layouts  2.4 us (2%)
    pallas_call x1, Pallas kernels, local(): pl.pallas_call(functools.partial(kernel, space, modes), out_shape=(jax.Sh...  108 us
    unnamed x4, local copies, waits for them, and re-layouts  2.4 us

profile of v4, /device:TPU:1, one launch (start us, length us, event | category | flops | bytes accessed | tf_op | source)
XLA Modules:
  0.0 111.4 jit_solution(6002960546354031893)
XLA Ops:
  0.6 108.4 %shard_map.113 = (f32[4,7,32,128]{3,2,1,0:T(8,128)}, f32[3,2,4]{2,1,0:T(2,128)}) custom-call(f32[7,32,128]{2,1,0:T(8,128)} %bitcast.20, f32[343,2,32]{2,1,0:T(2,128)} %bitcast.19, s32[6,32]{1,0:T(8,128)} %cols_hbm.1, s32[1,16]{1,0:T(1,128)} %bitcast.23, s32[1,128]{1,0:T(1,128)} %bitcast.24, s32[1,128]{1,0:T(1,128)} %bitcast.25, s32[1,256]{1,0:T(1,128)} %bitcast.22, ...), custom_call_target="tpu_custom_call" | custom-call | tf_op jit(solution)/shard_map/pallas_call | solution.py:630
  109.0 0.0 copy-start
  109.0 1.8 %copy.16 = f32[4,1,2,7,2048]{4,2,3,1,0:T(2,128)} copy(f32[4,1,2,7,2048]{4,2,3,1,0:T(2,128)} %bitcast.18) | data formatting | bytes 917504
  110.8 0.0 copy-done
  110.8 0.6 copy.17
Async XLA Ops:
  109.0 1.8 %copy-start = (f32[3,2,4]{2,1,0:T(2,128)S(1)}, f32[3,2,4]{2,1,0:T(2,128)}, u32[]{:S(2)}) copy-start(f32[3,2,4]{2,1,0:T(2,128)} %get-tuple-element.5) | copy-start | bytes 292
